TPU v7x, 256 devices: a whole 4x4x8 slice. The times are simulated.
256 devices in a mesh: prow: 16 (over z_hi, y), pcol: 16 (over z_lo, x, core).
Axes of the slice: x: 4, y: 4, z: 8 (z_hi: 4, z_lo: 2; z = z_hi * 2 + z_lo), core: 2. Of those that a mesh axis runs over, the one named last changes fastest.
Arguments:
- sigma_ancestors: float32 [16384, 16384], P('prow', 'pcol'), as said below
- panel_two: float32 [16384, 256], P('pcol'), may hold values from -0.0546875 to 0.0546875
- panel_one: float32 [16384, 256], P('pcol'), may hold values from -0.0625 to 0.0625
- panel_top: float32 [256, 256], replicated, may hold values from -0.375 to 0.375
- blocks_two: int32 [48], replicated, may hold values from 0 to 63, as said below
- blocks_one: int32 [32], replicated, may hold values from 0 to 63, as said below
- inverse_two: float32 [256, 256], replicated, as said below
- inverse_one: float32 [256, 256], replicated, as said below
Outputs:
- column_two: float32 [16384, 256], P('prow')
- diagonal_two: float32 [256, 256], replicated
- column_one: float32 [16384, 256], P('prow')
- coupling_one: float32 [256, 256], replicated
- diagonal_one: float32 [256, 256], replicated
Inputs may be any that keep to these rules, and one draw needn't show every extreme that they name: `blocks_two`: distinct and increasing; blocks 0, 32 and 63 are always listed. `blocks_one`: distinct and increasing, every one of them also listed in blocks_two; blocks 0, 32 and 63 are always listed. `sigma_ancestors`: symmetric positive definite. `inverse_two`: symmetric positive definite. `inverse_one`: symmetric positive definite.
All inputs are finite; a program needn't handle non-finite values.
Results may differ from a plain program's by a relative error of at most 0.000073.
Values sent between devices are 32-bit elements; how exact they have to be, the bound alone decides.
No kernel may reach another device: no remote copies, remote signals or barrier semaphores. Data moves between devices by JAX's collectives and lax.ppermute only.
A program may use at most 64 MiB of HBM per device.

v0:
```python
import functools

import jax
import jax.numpy as jnp
from jax import lax
from jax.experimental import pallas as pl
from jax.experimental.pallas import tpu as pltpu
from jax.sharding import Mesh, PartitionSpec as P

F32 = jnp.float32
BF16 = jnp.bfloat16
VMEM_LIMIT = 24 * 1024 * 1024
AXES = ("zh", "y", "zl", "x", "c")
SIZES = (4, 4, 2, 4, 2)
B = 256
W = 2 * B
CH = 64
CHIPS = 8
STEPS = 2
ROWS = 1024
HALF = 3 * B // 2
GR = HALF // CHIPS // 2
MM = ((1,), (0,))
TM = ((0,), (0,))
ROUTE = (
    0xCADEB16F, 0x52740983, 0xAEDC7695, 0x2F14803B, 0xBEF8C16D, 0x79A50432, 0x8EB91254, 0x3706FDAC,
    0x0218FDE7, 0x6453AC9B, 0x64315072, 0xDF8AEB9C, 0x29FB0341, 0xC567AED8, 0xC2513467, 0x08E9FDBA,
    0x43671025, 0xAE89CFDB, 0x46731052, 0x9AEFBC8D, 0x47561302, 0x98EDAFBC, 0x36407125, 0xCA9BFE8D,
    0x2430DEA1, 0xBC98F756, 0x421DBC8F, 0x5E9A3076, 0x0347E9AF, 0xD8CB5261, 0x6570F8DA, 0xB9CE2413,
)
SWAP = [(0, 1), (1, 0)]
VM = pl.BlockSpec(memory_space=pltpu.VMEM)
SM = pl.BlockSpec(memory_space=pltpu.SMEM)
HBM = pl.BlockSpec(memory_space=pltpu.HBM)
LONG = pl.CostEstimate(flops=20 << 30, bytes_accessed=8 << 20, transcendentals=0)
PARAMS = pltpu.CompilerParams(vmem_limit_bytes=VMEM_LIMIT)


def split(value):
    high = value.astype(BF16)
    return high, (value - high.astype(F32)).astype(BF16)


def dot3(left, right, dims):
    lh, ll = left
    rh, rl = right
    go = functools.partial(lax.dot_general, dimension_numbers=(dims, ((), ())), preferred_element_type=F32)
    return go(lh, rh) + (go(lh, rl) + go(ll, rh))


def in_hbm(value):
    return pltpu.with_memory_space_constraint(value, pltpu.HBM)


def flag(listed, block):
    return jnp.max(jnp.where(listed == block, 1.0, 0.0), axis=1, keepdims=True)


def product_rows(s_ref, low, high, z, p_ref):
    rows = split(s_ref[pl.ds(low, high - low)].reshape((high - low) * CH, ROWS))
    p_ref[pl.ds(low * CH, (high - low) * CH), :] = dot3(rows, z, MM)


def send_kernel(w_ref, s_hbm, two_hbm, one_hbm, top_hbm, b2_hbm, b1_hbm, p_ref, zh_ref, zl_ref, keep_ref,
                s_ref, two_ref, one_ref, top_ref, b2_ref, b1_ref, sems):
    per = CHIPS // STEPS
    blocks = ROWS // B

    def rows_of(core, i):
        return s_hbm.at[pl.ds(i * per, per), pl.ds(pl.multiple_of(core * CH, CH), CH), :]

    pairs = [(b2_hbm, b2_ref), (b1_hbm, b1_ref), (top_hbm, top_ref)]
    for k in range(blocks):
        rows = pl.ds(k * B, B)
        pairs += [(two_hbm.at[rows], two_ref.at[rows]), (one_hbm.at[rows], one_ref.at[rows])]
    for i in range(STEPS):
        pairs.append((rows_of(1 - w_ref[1], i), s_ref.at[pl.ds(i * per, per)]))
    for i in range(STEPS):
        pairs.append((rows_of(w_ref[1], i), keep_ref.at[pl.ds(i * per, per)]))
    copies = [pltpu.make_async_copy(src, dst, sems.at[i]) for i, (src, dst) in enumerate(pairs)]
    for copy in copies:
        copy.start()
    for copy in copies[:3]:
        copy.wait()
    top = split(top_ref[...])
    first = w_ref[0] * blocks
    for k in range(blocks):
        copies[3 + 2 * k].wait()
        copies[4 + 2 * k].wait()
        rows = pl.ds(k * B, B)
        live_two = two_ref[rows, :] * flag(b2_ref[...], first + k)
        live_one = one_ref[rows, :] * flag(b1_ref[...], first + k)
        h2, l2 = split(live_two)
        hw, lw = split(live_one - dot3((h2, l2), top, MM))
        zh_ref[rows, :B] = h2
        zl_ref[rows, :B] = l2
        zh_ref[rows, B:] = hw
        zl_ref[rows, B:] = lw
    z = (zh_ref[...], zl_ref[...])
    for i in range(STEPS):
        copies[3 + 2 * blocks + i].wait()
        product_rows(s_ref, i * per, (i + 1) * per, z, p_ref)
    for copy in copies[3 + 2 * blocks + STEPS:]:
        copy.wait()


def keep_kernel(s_ref, zh_ref, zl_ref, p_ref):
    z = (zh_ref[...], zl_ref[...])
    for i in range(STEPS):
        product_rows(s_ref, i * CHIPS // STEPS, (i + 1) * CHIPS // STEPS, z, p_ref)


def products(where, sigma, two, one, top, b2, b1, z_own):
    sigma = sigma.reshape(CHIPS, 2 * CH, ROWS)
    shape_p = jax.ShapeDtypeStruct((CHIPS * CH, W), F32)
    shape_z = jax.ShapeDtypeStruct((ROWS, W), BF16)
    shape_s = jax.ShapeDtypeStruct((CHIPS, CH, ROWS), F32)
    send, zh, zl, mine = pl.pallas_call(
        send_kernel,
        in_specs=[SM] + [HBM] * 6,
        out_specs=[VM] * 4,
        out_shape=[shape_p, shape_z, shape_z, shape_s],
        scratch_shapes=[
            pltpu.VMEM(shape_s.shape, F32),
            pltpu.VMEM((ROWS, B), F32),
            pltpu.VMEM((ROWS, B), F32),
            pltpu.VMEM((B, B), F32),
            pltpu.VMEM(b2.shape, jnp.int32),
            pltpu.VMEM(b1.shape, jnp.int32),
            pltpu.SemaphoreType.DMA((3 + 2 * (ROWS // B) + 2 * STEPS,)),
        ],
        compiler_params=PARAMS,
        cost_estimate=LONG,
        name="product_send",
    )(where, *map(in_hbm, (sigma, two, one, top, b2, b1)))

    got = lax.ppermute(send, "c", SWAP)
    keep = pl.pallas_call(
        keep_kernel,
        in_specs=[VM] * 3,
        out_specs=VM,
        out_shape=shape_p,
        compiler_params=PARAMS,
        cost_estimate=LONG,
        name="product_keep",
    )(mine, zh, zl)
    keep, z_own = lax.optimization_barrier((keep, z_own))
    pair = pl.pallas_call(
        add_kernel, in_specs=[VM] * 2, out_specs=VM, out_shape=shape_p, compiler_params=PARAMS, name="pair_sum"
    )(keep, got)
    return pair, z_own


def add_kernel(left_ref, right_ref, out_ref):
    out_ref[...] = left_ref[...] + right_ref[...]


def chunk_kernel(w_ref, own_ref, b2_ref, b1_ref, top_ref, inv2_ref, inv1_ref, chunk_ref, it_ref, base_ref):
    block = w_ref[2]
    two = own_ref[:, :B] * -flag(b2_ref[...], block)
    one = own_ref[:, B:] * -flag(b1_ref[...], block)
    for q in range(CHIPS):
        chunk_ref[pl.ds(q * CH, CH), :B] = two
        chunk_ref[pl.ds(q * CH, CH), B:] = one
    top = split(top_ref[...])
    it = dot3(split(inv2_ref[...]), top, MM)
    it_ref[...] = it
    base_ref[...] = inv1_ref[...] + dot3(top, split(it), TM)


def spread_kernel(own_ref, across_ref, ahead_ref, behind_ref, out_ref):
    total = (own_ref[...] + across_ref[...]) + (ahead_ref[...] + behind_ref[...])
    for q in range(CHIPS):
        out_ref[pl.ds(q * GR, GR), :] = total


def gram_kernel(w_ref, y_own_ref, y_oth_ref, z_own_ref, z_oth_ref, top_ref, b2_ref, b1_ref, g_ref):
    block = w_ref[2]
    f2 = flag(b2_ref[...], block)
    f1 = flag(b1_ref[...], block)
    own = y_own_ref[...]
    z = jnp.concatenate([z_own_ref[...], z_oth_ref[...]], axis=0)
    live_two = z[:, :B] * f2

    def place(parts):
        rows = 0
        for part in parts:
            for low in range(0, part.shape[0], 8):
                q, rest = divmod(rows + low, 2 * GR)
                h, row = divmod(rest, GR)
                g_ref[pl.ds(q * GR + row, 8), pl.ds(h * B, B)] = part[low:low + 8]
            rows += part.shape[0]

    @pl.when(w_ref[1] == 0)
    def _():
        y = split(jnp.concatenate([own, y_oth_ref[...]], axis=0))
        place((
            dot3(split(live_two), [v[:, :B] for v in y], TM),
            dot3(split(live_two[:, :B // 2]), [v[:, B:] for v in y], TM),
        ))

    @pl.when(w_ref[1] == 1)
    def _():
        y = split(jnp.concatenate([own[:, B:], y_oth_ref[:, B:]], axis=0))
        live_w = z[:, B:] * f1 - dot3(split(live_two), split(top_ref[...]), MM)
        place((dot3(split(live_two[:, B // 2:]), y, TM), dot3(split(live_w), y, TM)))


def assemble_kernel(w_ref, own_ref, oth_ref, c2_ref, c1_ref):
    mine = w_ref[1]
    for core, ref in ((mine, own_ref), (1 - mine, oth_ref)):
        for q in range(CHIPS):
            rows = pl.ds(pl.multiple_of(q * 2 * CH + core * CH, CH), CH)
            c2_ref[rows, :] = ref[pl.ds(q * CH, CH), :B]
            c1_ref[rows, :] = ref[pl.ds(q * CH, CH), B:]


def last_kernel(w_ref, own_ref, oth_ref, inv2_ref, it_ref, base_ref, d2_ref, cp_ref, d1_ref):
    def write(refs):
        for half, ref in enumerate(refs):
            for q in range(CHIPS):
                for h in range(2):
                    at = half * HALF + q * 2 * GR + h * GR
                    piece = ref[pl.ds(q * GR, GR), pl.ds(h * B, B)]
                    for low in range(0, GR, 8):
                        which, row = divmod(at + low, B)
                        rows = pl.ds(row, 8)
                        value = piece[low:low + 8]
                        if which == 0:
                            d2_ref[rows, :] = inv2_ref[rows, :] + value
                        elif which == 1:
                            cp_ref[rows, :] = value - it_ref[rows, :]
                        else:
                            d1_ref[rows, :] = base_ref[rows, :] + value

    @pl.when(w_ref[1] == 0)
    def _():
        write((own_ref, oth_ref))

    @pl.when(w_ref[1] == 1)
    def _():
        write((oth_ref, own_ref))


def route(i, j):
    return (ROUTE[2 * j + (i >> 3)] >> (4 * (i & 7))) & 15


def a2a(value, axes):
    return lax.all_to_all(value, axes, 0, 0, tiled=True)


def ring(value, axis):
    shift = lambda k: lax.ppermute(value, axis, [(i, (i + k) % 4) for i in range(4)])
    return value, shift(2), shift(1), shift(3)


def per_device(sigma, two, one, top, blocks_two, blocks_one, inv2, inv1):
    zh, y, zl, x, c = (lax.axis_index(a) for a in AXES)
    row = zh * 4 + y
    chip = zl * 4 + x
    where = jnp.stack([chip * 2 + c, c, row * 4 + lax.shift_right_logical(chip, 1)]).astype(jnp.int32)
    b2 = blocks_two.reshape(1, -1)
    b1 = blocks_one.reshape(1, -1)

    turn = [(i * 16 + j, j * 16 + route(i, j)) for i in range(16) for j in range(16)]
    word = jnp.uint32(ROUTE[0])
    for k, other in enumerate(ROUTE):
        word = jnp.where((chip * 2 + c) * 2 + lax.shift_right_logical(row, 3) == k, jnp.uint32(other), word)
    chunk = (lax.shift_right_logical(word, (4 * (row & 7)).astype(jnp.uint32)) & 15).astype(jnp.int32)
    part = jnp.concatenate([lax.dynamic_slice(p, (chunk * CH, 0), (CH, B)) for p in (two, one)], axis=1)
    z_own = lax.ppermute(part, AXES, turn)

    pair, z_own = products(where, sigma, two, one, top, b2, b1, z_own)
    y_parts = a2a(pair, ("zl", "x"))
    z_oth = lax.ppermute(z_own, "c", SWAP)

    own = jnp.sum(y_parts.reshape(CHIPS, CH, W), axis=0)
    oth = lax.ppermute(own, "c", SWAP)
    parts = jax.ShapeDtypeStruct((CHIPS * GR, W), F32)
    g = pl.pallas_call(
        gram_kernel,
        in_specs=[SM] + [VM] * 7,
        out_specs=VM,
        out_shape=parts,
        compiler_params=PARAMS,
        name="gram",
    )(where, own, oth, z_own, z_oth, top, b2, b1)
    g, y_own = lax.optimization_barrier((g, own))
    g = a2a(g, ("zl", "x"))
    square = jax.ShapeDtypeStruct((B, B), F32)
    chunks, it, base = pl.pallas_call(
        chunk_kernel,
        in_specs=[SM] + [VM] * 6,
        out_specs=[VM] * 3,
        out_shape=[jax.ShapeDtypeStruct((CHIPS * CH, W), F32), square, square],
        compiler_params=PARAMS,
        name="chunks",
    )(where, y_own, b2, b1, top, inv2, inv1)
    chunks = a2a(chunks, ("zl", "x"))

    g = jnp.sum(g.reshape(CHIPS, GR, W), axis=0)
    own, across, ahead, behind = ring(g, "y")
    g = ring((own + across) + (ahead + behind), "zh")
    g = pl.pallas_call(
        spread_kernel, in_specs=[VM] * 4, out_specs=VM, out_shape=parts, compiler_params=PARAMS, name="spread"
    )(*g)
    g = a2a(g, ("zl", "x"))

    column = jax.ShapeDtypeStruct((ROWS, B), F32)
    column_two, column_one = pl.pallas_call(
        assemble_kernel,
        in_specs=[SM] + [VM] * 2,
        out_specs=[VM] * 2,
        out_shape=[column] * 2,
        compiler_params=PARAMS,
        name="assemble",
    )(where, chunks, lax.ppermute(chunks, "c", SWAP))
    g_oth = lax.ppermute(g, "c", SWAP)
    base, column_two, column_one = lax.optimization_barrier((base, column_two, column_one))
    d2, cp, d1 = pl.pallas_call(
        last_kernel,
        in_specs=[SM] + [VM] * 5,
        out_specs=[VM] * 3,
        out_shape=[square] * 3,
        compiler_params=PARAMS,
        name="last",
    )(where, g, g_oth, inv2, it, base)

    return column_two, d2, column_one, cp, d1


def solution(mesh):
    fine = Mesh(mesh.devices.reshape(SIZES), AXES)
    prow = ("zh", "y")
    pcol = ("zl", "x", "c")
    in_specs = (P(prow, pcol), P(pcol, None), P(pcol, None), P(), P(), P(), P(), P())
    out_specs = (P(prow, None), P(), P(prow, None), P(), P())
    return jax.shard_map(
        per_device, mesh=fine, in_specs=in_specs, out_specs=out_specs, check_vma=False
    )
```

profile of v0, /device:TPU:1, one launch (start us, length us, event | category | flops | bytes accessed | tf_op | source)
XLA Modules:
  0.0 96.6 jit_solution(9081430965802402453)
XLA Ops:
  0.8 0.9 constant_dynamic-slice_fusion
  1.7 4.7 %collective-permute-start = (f32[64,512]{1,0:T(8,128)S(1)}, f32[64,512]{1,0:T(8,128)S(1)}, u32[]{:S(2)}, u32[]{:S(2)}) collective-permute-start(f32[64,512]{1,0:T(8,128)S(1)} %pad_maximum_fusion), channel_id=1, source_target_pairs={{0,15},{1,21},{2,45},{3,52},{4,71},{5,82},{6,97},{7,119},{8,133},{... | collective-permute-start | bytes 393224 | tf_op jit(solution)/shard_map/ppermute | solution.py:272
  6.4 0.1 pad_add_fusion.w_ref
  6.5 5.5 %product_send.1 = (f32[512,512]{1,0:T(8,128)S(1)}, bf16[1024,512]{1,0:T(8,128)(2,1)S(1)}, bf16[1024,512]{1,0:T(8,128)(2,1)S(1)}, f32[8,64,1024]{2,1,0:T(8,128)S(1)}) custom-call(s32[3]{0:T(128)S(1)} %pad_add_fusion.w_ref, f32[8,128,1024]{2,1,0:T(8,128)} %bitcast.22, f32[1024,256]{1,0:T(8,128)} %two_hbm.1, f32[1024,256]{1,0:T(8,128)} %one_hbm.1, ...), custom_call_target="tpu_custom_call" | custom-call | flops 21474836480 | bytes 8388608 | tf_op jit(solution)/shard_map/product_send/pallas_call | solution.py:118
  12.0 0.5 collective-permute-start.1
  12.5 1.8 %product_keep.1.left_ref = f32[512,512]{1,0:T(8,128)S(1)} custom-call(f32[8,64,1024]{2,1,0:T(8,128)S(1)} %get-tuple-element.24.s_ref, bf16[1024,512]{1,0:T(8,128)(2,1)S(1)} %get-tuple-element.25.zh_ref, bf16[1024,512]{1,0:T(8,128)(2,1)S(1)} %get-tuple-element.26.zl_ref), custom_call_target="tpu_custom_call" | custom-call | flops 21474836480 | bytes 8388608 | tf_op jit(solution)/shard_map/product_keep/pallas_call | solution.py:138
  14.3 0.0 copy-start
  14.4 0.0 copy-start.3
  14.4 0.0 copy-start.4
  14.4 0.0 copy-start.1
  14.4 0.0 copy-start.2
  14.4 0.0 collective-permute-done.z_own_ref
  14.4 0.4 collective-permute-done.1.right_ref
  14.8 1.1 %pair_sum.1 = f32[512,512]{1,0:T(8,128)} custom-call(f32[512,512]{1,0:T(8,128)S(1)} %product_keep.1.left_ref, f32[512,512]{1,0:T(8,128)S(1)} %collective-permute-done.1.right_ref), custom_call_target="tpu_custom_call" | custom-call | tf_op jit(solution)/shard_map/pair_sum/pallas_call | solution.py:148
  15.9 10.2 %all-to-all-start = ((f32[8,64,512]{2,1,0:T(8,128)}), f32[8,64,512]{2,1,0:T(8,128)S(1)}, u32[]{:S(2)}, u32[]{:S(2)}) async-start(f32[8,64,512]{2,1,0:T(8,128)} %bitcast.6), calls=%async_computation | async-start | bytes 2097152 | tf_op jit(solution)/shard_map/all_to_all | solution.py:250
  26.1 0.4 collective-permute-start.3
  26.6 14.6 %all-to-all-done = f32[8,64,512]{2,1,0:T(8,128)S(1)} async-done(((f32[8,64,512]{2,1,0:T(8,128)}), f32[8,64,512]{2,1,0:T(8,128)S(1)}, u32[]{:S(2)}, u32[]{:S(2)}) %all-to-all-start) | async-done | bytes 1048608 | tf_op jit(solution)/shard_map/all_to_all | solution.py:250
  41.1 0.1 reduce_sum.18.y_own_ref.own_ref
  41.2 0.9 collective-permute-start.2
  42.1 0.0 collective-permute-done.3.z_oth_ref
  42.1 1.0 %collective-permute-done.2.y_oth_ref = f32[64,512]{1,0:T(8,128)S(1)} collective-permute-done((f32[64,512]{1,0:T(8,128)S(1)}, f32[64,512]{1,0:T(8,128)S(1)}, u32[]{:S(2)}, u32[]{:S(2)}) %collective-permute-start.2) | collective-permute-done | bytes 131104 | tf_op jit(solution)/shard_map/ppermute | solution.py:279
  43.0 0.0 copy-done
  43.0 0.0 copy-done.3
  43.0 0.0 copy-done.4
  43.1 1.9 %gram.1 = f32[192,512]{1,0:T(8,128)} custom-call(s32[3]{0:T(128)S(1)} %pad_add_fusion.w_ref, f32[64,512]{1,0:T(8,128)S(1)} %reduce_sum.18.y_own_ref.own_ref, f32[64,512]{1,0:T(8,128)S(1)} %collective-permute-done.2.y_oth_ref, f32[64,512]{1,0:T(8,128)S(1)} %collective-permute-done.z_own_ref, f32[64,512]{1,0:T(8,128)S(1)} %collective-permute-done.3.z_oth_ref, ...), custom_call_target="tpu_custom_call" | custom-call | tf_op jit(solution)/shard_map/gram/pallas_call | solution.py:281
  45.0 3.5 %all-to-all-start.2 = ((f32[8,24,512]{2,1,0:T(8,128)}), f32[8,24,512]{2,1,0:T(8,128)S(1)}, u32[]{:S(2)}, u32[]{:S(2)}) async-start(f32[8,24,512]{2,1,0:T(8,128)} %bitcast.9), calls=%async_computation.2 | async-start | bytes 786432 | tf_op jit(solution)/shard_map/all_to_all | solution.py:250
  48.4 0.0 copy-done.1
  48.5 0.0 copy-done.2
  48.5 2.1 %chunks.1 = (f32[512,512]{1,0:T(8,128)}, f32[256,256]{1,0:T(8,128)S(1)}, f32[256,256]{1,0:T(8,128)S(1)}) custom-call(s32[3]{0:T(128)S(1)} %pad_add_fusion.w_ref, f32[64,512]{1,0:T(8,128)S(1)} %reduce_sum.18.y_own_ref.own_ref, s32[1,48]{1,0:T(1,128)S(1)} %bitcast.18, s32[1,32]{1,0:T(1,128)S(1)} %bitcast.21, f32[256,256]{1,0:T(8,128)S(1)} %copy-done, ...), custom_call_target="tpu_custom_call" | custom-call | tf_op jit(solution)/shard_map/chunks/pallas_call | solution.py:292
  50.6 5.1 %all-to-all-done.2 = f32[8,24,512]{2,1,0:T(8,128)S(1)} async-done(((f32[8,24,512]{2,1,0:T(8,128)}), f32[8,24,512]{2,1,0:T(8,128)S(1)}, u32[]{:S(2)}, u32[]{:S(2)}) %all-to-all-start.2) | async-done | bytes 393248 | tf_op jit(solution)/shard_map/all_to_all | solution.py:250
  55.7 4.2 %all-to-all-start.1 = ((f32[8,64,512]{2,1,0:T(8,128)}), f32[8,64,512]{2,1,0:T(8,128)S(1)}, u32[]{:S(2)}, u32[]{:S(2)}) async-start(f32[8,64,512]{2,1,0:T(8,128)} %bitcast.7), calls=%async_computation.1 | async-start | bytes 2097152 | tf_op jit(solution)/shard_map/all_to_all | solution.py:250
  60.0 0.1 collective-permute-start.6
  60.1 2.7 %collective-permute-start.7 = (f32[24,512]{1,0:T(8,128)S(1)}, f32[24,512]{1,0:T(8,128)S(1)}, u32[]{:S(2)}, u32[]{:S(2)}) collective-permute-start(f32[24,512]{1,0:T(8,128)S(1)} %reduce_sum.19), channel_id=1, source_target_pairs={{0,48},{16,0},{32,16},{48,32},{1,49},{17,1},{33,17},{49,33},{2,50}... | collective-permute-start | bytes 147464 | tf_op jit(solution)/shard_map/ppermute | solution.py:254
  62.7 0.0 collective-permute-start.5
  62.7 1.5 %collective-permute-done.6 = f32[24,512]{1,0:T(8,128)S(1)} collective-permute-done((f32[24,512]{1,0:T(8,128)S(1)}, f32[24,512]{1,0:T(8,128)S(1)}, u32[]{:S(2)}, u32[]{:S(2)}) %collective-permute-start.6) | collective-permute-done | bytes 49184 | tf_op jit(solution)/shard_map/ppermute | solution.py:254
  64.2 0.0 collective-permute-done.7
  64.2 3.3 %collective-permute-done.5 = f32[24,512]{1,0:T(8,128)S(1)} collective-permute-done((f32[24,512]{1,0:T(8,128)S(1)}, f32[24,512]{1,0:T(8,128)S(1)}, u32[]{:S(2)}, u32[]{:S(2)}) %collective-permute-start.5) | collective-permute-done | bytes 49184 | tf_op jit(solution)/shard_map/ppermute | solution.py:254
  67.5 1.2 %collective-permute-start.8 = (f32[24,512]{1,0:T(8,128)S(1)}, f32[24,512]{1,0:T(8,128)S(1)}, u32[]{:S(2)}, u32[]{:S(2)}) collective-permute-start(f32[24,512]{1,0:T(8,128)S(1)} %add_add_fusion.own_ref), channel_id=1, source_target_pairs={{0,128},{64,192},{128,0},{192,64},{1,129},{65,193},{129,1},{193,65... | collective-permute-start | bytes 147464 | tf_op jit(solution)/shard_map/ppermute | solution.py:254
  68.7 1.2 %collective-permute-start.9 = (f32[24,512]{1,0:T(8,128)S(1)}, f32[24,512]{1,0:T(8,128)S(1)}, u32[]{:S(2)}, u32[]{:S(2)}) collective-permute-start(f32[24,512]{1,0:T(8,128)S(1)} %add_add_fusion.own_ref), channel_id=1, source_target_pairs={{0,64},{64,128},{128,192},{192,0},{1,65},{65,129},{129,193},{193,1... | collective-permute-start | bytes 147464 | tf_op jit(solution)/shard_map/ppermute | solution.py:254
  69.8 2.4 %collective-permute-start.10 = (f32[24,512]{1,0:T(8,128)S(1)}, f32[24,512]{1,0:T(8,128)S(1)}, u32[]{:S(2)}, u32[]{:S(2)}) collective-permute-start(f32[24,512]{1,0:T(8,128)S(1)} %add_add_fusion.own_ref), channel_id=1, source_target_pairs={{0,192},{64,0},{128,64},{192,128},{1,193},{65,1},{129,65},{193,129... | collective-permute-start | bytes 147464 | tf_op jit(solution)/shard_map/ppermute | solution.py:254
  72.2 2.2 %collective-permute-done.8.across_ref = f32[24,512]{1,0:T(8,128)S(1)} collective-permute-done((f32[24,512]{1,0:T(8,128)S(1)}, f32[24,512]{1,0:T(8,128)S(1)}, u32[]{:S(2)}, u32[]{:S(2)}) %collective-permute-start.8) | collective-permute-done | bytes 49184 | tf_op jit(solution)/shard_map/ppermute | solution.py:254
  74.4 0.0 collective-permute-done.9.ahead_ref
  74.4 0.6 collective-permute-done.10.behind_ref
  75.0 0.8 spread.1
  75.8 0.0 all-to-all-done.1
  75.8 5.5 %all-to-all-start.3 = ((f32[8,24,512]{2,1,0:T(8,128)}), f32[8,24,512]{2,1,0:T(8,128)S(1)}, u32[]{:S(2)}, u32[]{:S(2)}) async-start(f32[8,24,512]{2,1,0:T(8,128)} %bitcast.10), calls=%async_computation.3 | async-start | bytes 786432 | tf_op jit(solution)/shard_map/all_to_all | solution.py:250
  81.2 4.0 %collective-permute-start.4 = (f32[512,512]{1,0:T(8,128)S(1)}, f32[512,512]{1,0:T(8,128)S(1)}, u32[]{:S(2)}, u32[]{:S(2)}) collective-permute-start(f32[512,512]{1,0:T(8,128)S(1)} %bitcast.12), channel_id=1, source_target_pairs={{0,1},{1,0},{2,3},{3,2},{4,5},{5,4},{6,7},{7,6},{8,9},{9,8},{10,11... | collective-permute-start | bytes 3145736 | tf_op jit(solution)/shard_map/ppermute | solution.py:318
  85.3 2.6 %all-to-all-done.3 = f32[8,24,512]{2,1,0:T(8,128)S(1)} async-done(((f32[8,24,512]{2,1,0:T(8,128)}), f32[8,24,512]{2,1,0:T(8,128)S(1)}, u32[]{:S(2)}, u32[]{:S(2)}) %all-to-all-start.3) | async-done | bytes 393248 | tf_op jit(solution)/shard_map/all_to_all | solution.py:250
  87.8 5.2 %collective-permute-start.11 = (f32[192,512]{1,0:T(8,128)S(1)}, f32[192,512]{1,0:T(8,128)S(1)}, u32[]{:S(2)}, u32[]{:S(2)}) collective-permute-start(f32[192,512]{1,0:T(8,128)S(1)} %bitcast.14), channel_id=1, source_target_pairs={{0,1},{1,0},{2,3},{3,2},{4,5},{5,4},{6,7},{7,6},{8,9},{9,8},{10,11... | collective-permute-start | bytes 1179656 | tf_op jit(solution)/shard_map/ppermute | solution.py:319
  93.0 0.0 collective-permute-done.4.oth_ref
  93.0 2.0 %assemble.1 = (f32[1024,256]{1,0:T(8,128)}, f32[1024,256]{1,0:T(8,128)}) custom-call(s32[3]{0:T(128)S(1)} %pad_add_fusion.w_ref, f32[512,512]{1,0:T(8,128)S(1)} %bitcast.13, f32[512,512]{1,0:T(8,128)S(1)} %collective-permute-done.4.oth_ref), custom_call_target="tpu_custom_call" | custom-call | tf_op jit(solution)/shard_map/assemble/pallas_call | solution.py:311
  95.0 0.0 collective-permute-done.11.oth_ref
  95.0 1.5 %last.1 = (f32[256,256]{1,0:T(8,128)}, f32[256,256]{1,0:T(8,128)}, f32[256,256]{1,0:T(8,128)}) custom-call(s32[3]{0:T(128)S(1)} %pad_add_fusion.w_ref, f32[192,512]{1,0:T(8,128)S(1)} %bitcast.15, f32[192,512]{1,0:T(8,128)S(1)} %collective-permute-done.11.oth_ref, f32[256,256]{1,0:T(8,128)S(1)} %copy-done.1, f32[256,256]{1,0:T(8,128)S(1)} %get-tuple-element.37.it_ref, ...), custom_call_target="tpu_custom_call" | custom-call | tf_op jit(solution)/shard_map/last/pallas_call | solution.py:321
  (3 shorter events, 0.1 us)
Async XLA Ops:
  1.7 12.7 %collective-permute-start = (f32[64,512]{1,0:T(8,128)S(1)}, f32[64,512]{1,0:T(8,128)S(1)}, u32[]{:S(2)}, u32[]{:S(2)}) collective-permute-start(f32[64,512]{1,0:T(8,128)S(1)} %pad_maximum_fusion), channel_id=1, source_target_pairs={{0,15},{1,21},{2,45},{3,52},{4,71},{5,82},{6,97},{7,119},{8,133},{... | collective-permute-start | bytes 393224 | tf_op jit(solution)/shard_map/ppermute | solution.py:272
  12.0 2.8 %collective-permute-start.1 = (f32[512,512]{1,0:T(8,128)S(1)}, f32[512,512]{1,0:T(8,128)S(1)}, u32[]{:S(2)}, u32[]{:S(2)}) collective-permute-start(f32[512,512]{1,0:T(8,128)S(1)} %get-tuple-element.28), channel_id=1, source_target_pairs={{0,1},{1,0},{2,3},{3,2},{4,5},{5,4},{6,7},{7,6},{8,9},{9,8},{10,11... | collective-permute-start | bytes 3145736 | tf_op jit(solution)/shard_map/ppermute | solution.py:137
  14.3 28.7 %copy-start = (f32[256,256]{1,0:T(8,128)S(1)}, f32[256,256]{1,0:T(8,128)}, u32[]{:S(2)}) copy-start(f32[256,256]{1,0:T(8,128)} %top_ref.3) | copy-start | bytes 786436
  14.4 28.7 %copy-start.3 = (s32[48]{0:T(128)S(1)}, s32[48]{0:T(128)}, u32[]{:S(2)}) copy-start(s32[48]{0:T(128)} %param.12) | copy-start | bytes 580
  14.4 28.7 %copy-start.4 = (s32[32]{0:T(128)S(1)}, s32[32]{0:T(128)}, u32[]{:S(2)}) copy-start(s32[32]{0:T(128)} %param.13) | copy-start | bytes 388
  14.4 34.1 %copy-start.1 = (f32[256,256]{1,0:T(8,128)S(1)}, f32[256,256]{1,0:T(8,128)}, u32[]{:S(2)}) copy-start(f32[256,256]{1,0:T(8,128)} %inv2_ref.3) | copy-start | bytes 786436
  14.4 34.1 %copy-start.2 = (f32[256,256]{1,0:T(8,128)S(1)}, f32[256,256]{1,0:T(8,128)}, u32[]{:S(2)}) copy-start(f32[256,256]{1,0:T(8,128)} %inv1_ref.1) | copy-start | bytes 786436
  15.9 25.2 %all-to-all-start = ((f32[8,64,512]{2,1,0:T(8,128)}), f32[8,64,512]{2,1,0:T(8,128)S(1)}, u32[]{:S(2)}, u32[]{:S(2)}) async-start(f32[8,64,512]{2,1,0:T(8,128)} %bitcast.6), calls=%async_computation | async-start | bytes 2097152 | tf_op jit(solution)/shard_map/all_to_all | solution.py:250
  26.1 15.9 %collective-permute-start.3 = (f32[64,512]{1,0:T(8,128)S(1)}, f32[64,512]{1,0:T(8,128)S(1)}, u32[]{:S(2)}, u32[]{:S(2)}) collective-permute-start(f32[64,512]{1,0:T(8,128)S(1)} %collective-permute-done.z_own_ref), channel_id=1, source_target_pairs={{0,1},{1,0},{2,3},{3,2},{4,5},{5,4},{6,7},{7,6},{8,9},{9,8},{10,11... | collective-permute-start | bytes 393224 | tf_op jit(solution)/shard_map/ppermute | solution.py:276
  41.2 1.8 %collective-permute-start.2 = (f32[64,512]{1,0:T(8,128)S(1)}, f32[64,512]{1,0:T(8,128)S(1)}, u32[]{:S(2)}, u32[]{:S(2)}) collective-permute-start(f32[64,512]{1,0:T(8,128)S(1)} %reduce_sum.18.y_own_ref.own_ref), channel_id=1, source_target_pairs={{0,1},{1,0},{2,3},{3,2},{4,5},{5,4},{6,7},{7,6},{8,9},{9,8},{10,11... | collective-permute-start | bytes 393224 | tf_op jit(solution)/shard_map/ppermute | solution.py:279
  45.0 10.8 %all-to-all-start.2 = ((f32[8,24,512]{2,1,0:T(8,128)}), f32[8,24,512]{2,1,0:T(8,128)S(1)}, u32[]{:S(2)}, u32[]{:S(2)}) async-start(f32[8,24,512]{2,1,0:T(8,128)} %bitcast.9), calls=%async_computation.2 | async-start | bytes 786432 | tf_op jit(solution)/shard_map/all_to_all | solution.py:250
  55.7 20.0 %all-to-all-start.1 = ((f32[8,64,512]{2,1,0:T(8,128)}), f32[8,64,512]{2,1,0:T(8,128)S(1)}, u32[]{:S(2)}, u32[]{:S(2)}) async-start(f32[8,64,512]{2,1,0:T(8,128)} %bitcast.7), calls=%async_computation.1 | async-start | bytes 2097152 | tf_op jit(solution)/shard_map/all_to_all | solution.py:250
  60.0 4.2 %collective-permute-start.6 = (f32[24,512]{1,0:T(8,128)S(1)}, f32[24,512]{1,0:T(8,128)S(1)}, u32[]{:S(2)}, u32[]{:S(2)}) collective-permute-start(f32[24,512]{1,0:T(8,128)S(1)} %reduce_sum.19), channel_id=1, source_target_pairs={{0,16},{16,32},{32,48},{48,0},{1,17},{17,33},{33,49},{49,1},{2,18}... | collective-permute-start | bytes 147464 | tf_op jit(solution)/shard_map/ppermute | solution.py:254
  60.1 4.1 %collective-permute-start.7 = (f32[24,512]{1,0:T(8,128)S(1)}, f32[24,512]{1,0:T(8,128)S(1)}, u32[]{:S(2)}, u32[]{:S(2)}) collective-permute-start(f32[24,512]{1,0:T(8,128)S(1)} %reduce_sum.19), channel_id=1, source_target_pairs={{0,48},{16,0},{32,16},{48,32},{1,49},{17,1},{33,17},{49,33},{2,50}... | collective-permute-start | bytes 147464 | tf_op jit(solution)/shard_map/ppermute | solution.py:254
  62.7 4.7 %collective-permute-start.5 = (f32[24,512]{1,0:T(8,128)S(1)}, f32[24,512]{1,0:T(8,128)S(1)}, u32[]{:S(2)}, u32[]{:S(2)}) collective-permute-start(f32[24,512]{1,0:T(8,128)S(1)} %reduce_sum.19), channel_id=1, source_target_pairs={{0,32},{16,48},{32,0},{48,16},{1,33},{17,49},{33,1},{49,17},{2,34}... | collective-permute-start | bytes 147464 | tf_op jit(solution)/shard_map/ppermute | solution.py:254
  67.5 6.9 %collective-permute-start.8 = (f32[24,512]{1,0:T(8,128)S(1)}, f32[24,512]{1,0:T(8,128)S(1)}, u32[]{:S(2)}, u32[]{:S(2)}) collective-permute-start(f32[24,512]{1,0:T(8,128)S(1)} %add_add_fusion.own_ref), channel_id=1, source_target_pairs={{0,128},{64,192},{128,0},{192,64},{1,129},{65,193},{129,1},{193,65... | collective-permute-start | bytes 147464 | tf_op jit(solution)/shard_map/ppermute | solution.py:254
  68.7 5.8 %collective-permute-start.9 = (f32[24,512]{1,0:T(8,128)S(1)}, f32[24,512]{1,0:T(8,128)S(1)}, u32[]{:S(2)}, u32[]{:S(2)}) collective-permute-start(f32[24,512]{1,0:T(8,128)S(1)} %add_add_fusion.own_ref), channel_id=1, source_target_pairs={{0,64},{64,128},{128,192},{192,0},{1,65},{65,129},{129,193},{193,1... | collective-permute-start | bytes 147464 | tf_op jit(solution)/shard_map/ppermute | solution.py:254
  69.8 5.2 %collective-permute-start.10 = (f32[24,512]{1,0:T(8,128)S(1)}, f32[24,512]{1,0:T(8,128)S(1)}, u32[]{:S(2)}, u32[]{:S(2)}) collective-permute-start(f32[24,512]{1,0:T(8,128)S(1)} %add_add_fusion.own_ref), channel_id=1, source_target_pairs={{0,192},{64,0},{128,64},{192,128},{1,193},{65,1},{129,65},{193,129... | collective-permute-start | bytes 147464 | tf_op jit(solution)/shard_map/ppermute | solution.py:254
  75.8 12.1 %all-to-all-start.3 = ((f32[8,24,512]{2,1,0:T(8,128)}), f32[8,24,512]{2,1,0:T(8,128)S(1)}, u32[]{:S(2)}, u32[]{:S(2)}) async-start(f32[8,24,512]{2,1,0:T(8,128)} %bitcast.10), calls=%async_computation.3 | async-start | bytes 786432 | tf_op jit(solution)/shard_map/all_to_all | solution.py:250
  81.2 11.8 %collective-permute-start.4 = (f32[512,512]{1,0:T(8,128)S(1)}, f32[512,512]{1,0:T(8,128)S(1)}, u32[]{:S(2)}, u32[]{:S(2)}) collective-permute-start(f32[512,512]{1,0:T(8,128)S(1)} %bitcast.12), channel_id=1, source_target_pairs={{0,1},{1,0},{2,3},{3,2},{4,5},{5,4},{6,7},{7,6},{8,9},{9,8},{10,11... | collective-permute-start | bytes 3145736 | tf_op jit(solution)/shard_map/ppermute | solution.py:318
  87.8 7.2 %collective-permute-start.11 = (f32[192,512]{1,0:T(8,128)S(1)}, f32[192,512]{1,0:T(8,128)S(1)}, u32[]{:S(2)}, u32[]{:S(2)}) collective-permute-start(f32[192,512]{1,0:T(8,128)S(1)} %bitcast.14), channel_id=1, source_target_pairs={{0,1},{1,0},{2,3},{3,2},{4,5},{5,4},{6,7},{7,6},{8,9},{9,8},{10,11... | collective-permute-start | bytes 1179656 | tf_op jit(solution)/shard_map/ppermute | solution.py:319
where the time goes:
time: 97 us; the launch traced here: 96.6 us
  starting transfers between devices  46.5 us (48%)
  waiting for transfers between devices  31.2 us (32%)
  Pallas kernels  16.8 us (17%)
    all_to_all x4, starting transfers between devices, a2a(): return lax.all_to_all(value, axes, 0, 0, tiled=True)  23.3 us
    all_to_all x4, waiting for transfers between devices, a2a(): return lax.all_to_all(value, axes, 0, 0, tiled=True)  22.3 us
    ppermute x6, waiting for transfers between devices, ring(): lax.ppermute(value, axis, [(i, (i + k) % 4) for i in range(4)])  7.51 us
    ppermute x6, starting transfers between devices, ring(): lax.ppermute(value, axis, [(i, (i + k) % 4) for i in range(4)])  7.49 us
    pallas_call x1, Pallas kernels, products(): pl.pallas_call(send_kernel, in_specs=[SM] + [HBM] * 6, out_specs=[VM] * 4...  5.54 us
    ppermute x1, starting transfers between devices, per_device(): g_oth = lax.ppermute(g, 'c', SWAP)  5.18 us
    ppermute x1, starting transfers between devices, per_device(): z_own = lax.ppermute(part, AXES, turn)  4.67 us
    ppermute x1, starting transfers between devices, per_device(): lax.ppermute(chunks, 'c', SWAP)  4.03 us
  transfers between devices with their start and end apart: 16, of which 9 were waited for; matrix products, arithmetic and copies ran while one was open for 0% of the time, Pallas kernels for 13%

commit v1 on v0

--- a/solution.py
+++ b/solution.py
@@ -33,6 +33,7 @@
 SM = pl.BlockSpec(memory_space=pltpu.SMEM)
 HBM = pl.BlockSpec(memory_space=pltpu.HBM)
 LONG = pl.CostEstimate(flops=20 << 30, bytes_accessed=8 << 20, transcendentals=0)
+LONGER = pl.CostEstimate(flops=20 << 30, bytes_accessed=8 << 20, transcendentals=0)
 PARAMS = pltpu.CompilerParams(vmem_limit_bytes=VMEM_LIMIT)
 
 
@@ -61,7 +62,7 @@
     p_ref[pl.ds(low * CH, (high - low) * CH), :] = dot3(rows, z, MM)
 
 
-def send_kernel(w_ref, s_hbm, two_hbm, one_hbm, top_hbm, b2_hbm, b1_hbm, p_ref, zh_ref, zl_ref, keep_ref,
+def send_kernel(w_ref, s_hbm, two_hbm, one_hbm, top_hbm, b2_hbm, b1_hbm, p_ref, zh_ref, zl_ref, keep_ref, part_ref,
                 s_ref, two_ref, one_ref, top_ref, b2_ref, b1_ref, sems):
     per = CHIPS // STEPS
     blocks = ROWS // B
@@ -96,6 +97,9 @@
         zl_ref[rows, :B] = l2
         zh_ref[rows, B:] = hw
         zl_ref[rows, B:] = lw
+    chunk = pl.ds(pl.multiple_of(w_ref[3] * CH, CH), CH)
+    part_ref[:, :B] = two_ref[chunk, :]
+    part_ref[:, B:] = one_ref[chunk, :]
     z = (zh_ref[...], zl_ref[...])
     for i in range(STEPS):
         copies[3 + 2 * blocks + i].wait()
@@ -110,16 +114,16 @@
         product_rows(s_ref, i * CHIPS // STEPS, (i + 1) * CHIPS // STEPS, z, p_ref)
 
 
-def products(where, sigma, two, one, top, b2, b1, z_own):
+def products(where, sigma, two, one, top, b2, b1):
     sigma = sigma.reshape(CHIPS, 2 * CH, ROWS)
     shape_p = jax.ShapeDtypeStruct((CHIPS * CH, W), F32)
     shape_z = jax.ShapeDtypeStruct((ROWS, W), BF16)
     shape_s = jax.ShapeDtypeStruct((CHIPS, CH, ROWS), F32)
-    send, zh, zl, mine = pl.pallas_call(
+    send, zh, zl, mine, part = pl.pallas_call(
         send_kernel,
         in_specs=[SM] + [HBM] * 6,
-        out_specs=[VM] * 4,
-        out_shape=[shape_p, shape_z, shape_z, shape_s],
+        out_specs=[VM] * 5,
+        out_shape=[shape_p, shape_z, shape_z, shape_s, jax.ShapeDtypeStruct((CH, W), F32)],
         scratch_shapes=[
             pltpu.VMEM(shape_s.shape, F32),
             pltpu.VMEM((ROWS, B), F32),
@@ -144,11 +148,34 @@
         cost_estimate=LONG,
         name="product_keep",
     )(mine, zh, zl)
-    keep, z_own = lax.optimization_barrier((keep, z_own))
     pair = pl.pallas_call(
         add_kernel, in_specs=[VM] * 2, out_specs=VM, out_shape=shape_p, compiler_params=PARAMS, name="pair_sum"
     )(keep, got)
-    return pair, z_own
+    return pair, part
+
+
+def sum_kernel(parts, in_ref, after_ref, out_ref):
+    rows = out_ref.shape[0]
+    total = in_ref[pl.ds(0, rows), :]
+    for k in range(1, parts):
+        total = total + in_ref[pl.ds(k * rows, rows), :]
+    out_ref[...] = total
+
+
+def sum_parts(value, after):
+    rows = value.shape[0] // CHIPS
+    return pl.pallas_call(
+        functools.partial(sum_kernel, CHIPS),
+        in_specs=[VM, pl.BlockSpec(memory_space=pl.ANY)],
+        out_specs=VM,
+        out_shape=jax.ShapeDtypeStruct((rows, W), F32),
+        compiler_params=PARAMS,
+        name="sum_parts",
+    )(value, after)
+
+
+def ring_kernel(own_ref, behind_ref, ahead_ref, across_ref, out_ref):
+    out_ref[...] = (own_ref[...] + across_ref[...]) + (ahead_ref[...] + behind_ref[...])
 
 
 def add_kernel(left_ref, right_ref, out_ref):
@@ -168,20 +195,21 @@
     base_ref[...] = inv1_ref[...] + dot3(top, split(it), TM)
 
 
-def spread_kernel(own_ref, across_ref, ahead_ref, behind_ref, out_ref):
+def spread_kernel(own_ref, behind_ref, ahead_ref, across_ref, out_ref):
     total = (own_ref[...] + across_ref[...]) + (ahead_ref[...] + behind_ref[...])
     for q in range(CHIPS):
         out_ref[pl.ds(q * GR, GR), :] = total
 
 
-def gram_kernel(w_ref, y_own_ref, y_oth_ref, z_own_ref, z_oth_ref, top_ref, b2_ref, b1_ref, g_ref):
+def rows_kernel(w_ref, z_ref, top_ref, b2_ref, b1_ref, live_ref):
     block = w_ref[2]
-    f2 = flag(b2_ref[...], block)
-    f1 = flag(b1_ref[...], block)
-    own = y_own_ref[...]
-    z = jnp.concatenate([z_own_ref[...], z_oth_ref[...]], axis=0)
-    live_two = z[:, :B] * f2
-
+    live_two = z_ref[:, :B] * flag(b2_ref[...], block)
+    live_one = z_ref[:, B:] * flag(b1_ref[...], block)
+    live_ref[:, :B] = live_two
+    live_ref[:, B:] = live_one - dot3(split(live_two), split(top_ref[...]), MM)
+
+
+def gram_kernel(w_ref, own_ref, oth_ref, z_own_ref, z_oth_ref, g_ref):
     def place(parts):
         rows = 0
         for part in parts:
@@ -191,19 +219,23 @@
                 g_ref[pl.ds(q * GR + row, 8), pl.ds(h * B, B)] = part[low:low + 8]
             rows += part.shape[0]
 
+    z = split(jnp.concatenate([z_own_ref[...], z_oth_ref[...]], axis=0))
+
+    def columns(pair, low, high):
+        return [v[:, low:high] for v in pair]
+
     @pl.when(w_ref[1] == 0)
     def _():
-        y = split(jnp.concatenate([own, y_oth_ref[...]], axis=0))
+        y = split(jnp.concatenate([own_ref[...], oth_ref[...]], axis=0))
         place((
-            dot3(split(live_two), [v[:, :B] for v in y], TM),
-            dot3(split(live_two[:, :B // 2]), [v[:, B:] for v in y], TM),
+            dot3(columns(z, 0, B), columns(y, 0, B), TM),
+            dot3(columns(z, 0, B // 2), columns(y, B, W), TM),
         ))
 
     @pl.when(w_ref[1] == 1)
     def _():
-        y = split(jnp.concatenate([own[:, B:], y_oth_ref[:, B:]], axis=0))
-        live_w = z[:, B:] * f1 - dot3(split(live_two), split(top_ref[...]), MM)
-        place((dot3(split(live_two[:, B // 2:]), y, TM), dot3(split(live_w), y, TM)))
+        y = split(jnp.concatenate([own_ref[:, B:], oth_ref[:, B:]], axis=0))
+        place((dot3(columns(z, B // 2, B), y, TM), dot3(columns(z, B, W), y, TM)))
 
 
 def assemble_kernel(w_ref, own_ref, oth_ref, c2_ref, c1_ref):
@@ -252,14 +284,13 @@
 
 def ring(value, axis):
     shift = lambda k: lax.ppermute(value, axis, [(i, (i + k) % 4) for i in range(4)])
-    return value, shift(2), shift(1), shift(3)
+    return value, shift(3), shift(1), shift(2)
 
 
 def per_device(sigma, two, one, top, blocks_two, blocks_one, inv2, inv1):
-    zh, y, zl, x, c = (lax.axis_index(a) for a in AXES)
-    row = zh * 4 + y
-    chip = zl * 4 + x
-    where = jnp.stack([chip * 2 + c, c, row * 4 + lax.shift_right_logical(chip, 1)]).astype(jnp.int32)
+    z_hi, y, z_lo, x, c = (lax.axis_index(a) for a in AXES)
+    row = z_hi * 4 + y
+    chip = z_lo * 4 + x
     b2 = blocks_two.reshape(1, -1)
     b1 = blocks_one.reshape(1, -1)
 
@@ -268,24 +299,31 @@
     for k, other in enumerate(ROUTE):
         word = jnp.where((chip * 2 + c) * 2 + lax.shift_right_logical(row, 3) == k, jnp.uint32(other), word)
     chunk = (lax.shift_right_logical(word, (4 * (row & 7)).astype(jnp.uint32)) & 15).astype(jnp.int32)
-    part = jnp.concatenate([lax.dynamic_slice(p, (chunk * CH, 0), (CH, B)) for p in (two, one)], axis=1)
+    where = jnp.stack([chip * 2 + c, c, row * 4 + lax.shift_right_logical(chip, 1), chunk]).astype(jnp.int32)
+    pair, part = products(where, sigma, two, one, top, b2, b1)
     z_own = lax.ppermute(part, AXES, turn)
-
-    pair, z_own = products(where, sigma, two, one, top, b2, b1, z_own)
     y_parts = a2a(pair, ("zl", "x"))
+    z_own = pl.pallas_call(
+        rows_kernel,
+        in_specs=[SM] + [VM] * 4,
+        out_specs=VM,
+        out_shape=jax.ShapeDtypeStruct((CH, W), F32),
+        compiler_params=PARAMS,
+        cost_estimate=LONGER,
+        name="panel_rows",
+    )(where, z_own, top, b2, b1)
     z_oth = lax.ppermute(z_own, "c", SWAP)
-
-    own = jnp.sum(y_parts.reshape(CHIPS, CH, W), axis=0)
+    own = sum_parts(y_parts, z_own)
     oth = lax.ppermute(own, "c", SWAP)
     parts = jax.ShapeDtypeStruct((CHIPS * GR, W), F32)
     g = pl.pallas_call(
         gram_kernel,
-        in_specs=[SM] + [VM] * 7,
+        in_specs=[SM] + [VM] * 4,
         out_specs=VM,
         out_shape=parts,
         compiler_params=PARAMS,
         name="gram",
-    )(where, own, oth, z_own, z_oth, top, b2, b1)
+    )(where, own, oth, z_own, z_oth)
     g, y_own = lax.optimization_barrier((g, own))
     g = a2a(g, ("zl", "x"))
     square = jax.ShapeDtypeStruct((B, B), F32)
@@ -299,9 +337,12 @@
     )(where, y_own, b2, b1, top, inv2, inv1)
     chunks = a2a(chunks, ("zl", "x"))
 
-    g = jnp.sum(g.reshape(CHIPS, GR, W), axis=0)
-    own, across, ahead, behind = ring(g, "y")
-    g = ring((own + across) + (ahead + behind), "zh")
+    g = sum_parts(g, base)
+    g = pl.pallas_call(
+        ring_kernel, in_specs=[VM] * 4, out_specs=VM, out_shape=jax.ShapeDtypeStruct((GR, W), F32),
+        compiler_params=PARAMS, name="ring_sum",
+    )(*ring(g, "y"))
+    g = ring(g, "zh")
     g = pl.pallas_call(
         spread_kernel, in_specs=[VM] * 4, out_specs=VM, out_shape=parts, compiler_params=PARAMS, name="spread"
     )(*g)

time: 97 us -> 94.1 us (0.970)
  waiting for transfers between devices: 31.2 us -> 28.6 us
    ppermute x6, waiting for transfers between devices: 7.51 us -> 5.94 us  [ring(): lax.ppermute(value, axis, [(i, (i + k) % 4) for i in range(4)])]
    all_to_all x4, waiting for transfers between devices: 22.3 us -> 21.2 us  [a2a(): return lax.all_to_all(value, axes, 0, 0, tiled=True)]
    pallas_call x2 -> x6, Pallas kernels: 7.47 us -> 8.11 us  [the longest x1 5.55 us: products(): pl.pallas_call(send_kernel, in_specs=[SM] + [HBM] * 6, out_specs=[VM] * 5...]
  transfers between devices with their start and end apart: 16 -> 16, of which waited for: 9 -> 9; matrix products, arithmetic and copies ran while one was open for 0% -> 0% of each run, Pallas kernels for 13% -> 9%
where the time goes in v1:
time: 94.1 us; the launch traced here: 93.7 us
  starting transfers between devices  46.6 us (50%)
  waiting for transfers between devices  28.6 us (30%)
  Pallas kernels  17.4 us (18%)
    all_to_all x4, starting transfers between devices, a2a(): return lax.all_to_all(value, axes, 0, 0, tiled=True)  23.2 us
    all_to_all x4, waiting for transfers between devices, a2a(): return lax.all_to_all(value, axes, 0, 0, tiled=True)  21.2 us
    ppermute x6, starting transfers between devices, ring(): lax.ppermute(value, axis, [(i, (i + k) % 4) for i in range(4)])  8.32 us
    ppermute x6, waiting for transfers between devices, ring(): lax.ppermute(value, axis, [(i, (i + k) % 4) for i in range(4)])  5.94 us
    pallas_call x1, Pallas kernels, products(): pl.pallas_call(send_kernel, in_specs=[SM] + [HBM] * 6, out_specs=[VM] * 5...  5.55 us
    ppermute x1, starting transfers between devices, per_device(): g_oth = lax.ppermute(g, 'c', SWAP)  4.86 us
    ppermute x1, starting transfers between devices, per_device(): z_own = lax.ppermute(part, AXES, turn)  4.67 us
    ppermute x1, starting transfers between devices, per_device(): lax.ppermute(chunks, 'c', SWAP)  3.71 us
  transfers between devices with their start and end apart: 16, of which 9 were waited for; matrix products, arithmetic and copies ran while one was open for 0% of the time, Pallas kernels for 9%

profile of v1, /device:TPU:1, one launch (start us, length us, event | category | flops | bytes accessed | tf_op | source)
XLA Modules:
  0.0 93.7 jit_solution(9418783113650267573)
XLA Ops:
  0.8 0.1 pad_add_fusion.w_ref
  0.9 5.6 %product_send.1 = (f32[512,512]{1,0:T(8,128)S(1)}, bf16[1024,512]{1,0:T(8,128)(2,1)S(1)}, bf16[1024,512]{1,0:T(8,128)(2,1)S(1)}, f32[8,64,1024]{2,1,0:T(8,128)S(1)}, f32[64,512]{1,0:T(8,128)S(1)}) custom-call(s32[4]{0:T(128)S(1)} %pad_add_fusion.w_ref, f32[8,128,1024]{2,1,0:T(8,128)} %bitcast.27, f32[1024,256]{1,0:T(8,128)} %two_hbm.1, f32[1024,256]{1,0:T(8,128)} %one_hbm.1, ...), custom_call_target="tpu_custom_call" | custom-call | flops 21474836480 | bytes 8388608 | tf_op jit(solution)/shard_map/product_send/pallas_call | solution.py:122
  6.4 4.7 %collective-permute-start.1 = (f32[64,512]{1,0:T(8,128)S(1)}, f32[64,512]{1,0:T(8,128)S(1)}, u32[]{:S(2)}, u32[]{:S(2)}) collective-permute-start(f32[64,512]{1,0:T(8,128)S(1)} %get-tuple-element.27), channel_id=1, source_target_pairs={{0,15},{1,21},{2,45},{3,52},{4,71},{5,82},{6,97},{7,119},{8,133},{... | collective-permute-start | bytes 393224 | tf_op jit(solution)/shard_map/ppermute | solution.py:304
  11.1 0.5 collective-permute-start
  11.6 1.8 %product_keep.1.left_ref = f32[512,512]{1,0:T(8,128)S(1)} custom-call(f32[8,64,1024]{2,1,0:T(8,128)S(1)} %get-tuple-element.23.s_ref, bf16[1024,512]{1,0:T(8,128)(2,1)S(1)} %get-tuple-element.24.zh_ref, bf16[1024,512]{1,0:T(8,128)(2,1)S(1)} %get-tuple-element.25.zl_ref), custom_call_target="tpu_custom_call" | custom-call | flops 21474836480 | bytes 8388608 | tf_op jit(solution)/shard_map/product_keep/pallas_call | solution.py:142
  13.4 0.0 copy-start.1
  13.4 0.0 copy-start.3
  13.4 0.0 copy-start.4
  13.4 0.5 collective-permute-done.right_ref
  13.8 1.1 %pair_sum.1 = f32[512,512]{1,0:T(8,128)} custom-call(f32[512,512]{1,0:T(8,128)S(1)} %product_keep.1.left_ref, f32[512,512]{1,0:T(8,128)S(1)} %collective-permute-done.right_ref), custom_call_target="tpu_custom_call" | custom-call | tf_op jit(solution)/shard_map/pair_sum/pallas_call | solution.py:151
  14.9 10.2 %all-to-all-start = ((f32[8,64,512]{2,1,0:T(8,128)}), f32[8,64,512]{2,1,0:T(8,128)S(1)}, u32[]{:S(2)}, u32[]{:S(2)}) async-start(f32[8,64,512]{2,1,0:T(8,128)} %bitcast.7), calls=%async_computation | async-start | bytes 2097152 | tf_op jit(solution)/shard_map/all_to_all | solution.py:282
  25.1 0.0 copy-start
  25.2 0.0 copy-start.2
  25.2 0.0 collective-permute-done.1.z_ref
  25.2 0.0 copy-done.1
  25.2 0.0 copy-done.3
  25.2 0.0 copy-done.4
  25.2 0.8 panel_rows.1.after_ref.z_own_ref
  26.0 0.5 collective-permute-start.3
  26.5 13.6 %all-to-all-done = f32[8,64,512]{2,1,0:T(8,128)S(1)} async-done(((f32[8,64,512]{2,1,0:T(8,128)}), f32[8,64,512]{2,1,0:T(8,128)S(1)}, u32[]{:S(2)}, u32[]{:S(2)}) %all-to-all-start) | async-done | bytes 1048608 | tf_op jit(solution)/shard_map/all_to_all | solution.py:282
  40.1 0.1 sum_parts.2.own_ref
  40.2 0.9 collective-permute-start.2
  41.0 0.0 collective-permute-done.3.z_oth_ref
  41.0 1.0 %collective-permute-done.2.oth_ref = f32[64,512]{1,0:T(8,128)S(1)} collective-permute-done((f32[64,512]{1,0:T(8,128)S(1)}, f32[64,512]{1,0:T(8,128)S(1)}, u32[]{:S(2)}, u32[]{:S(2)}) %collective-permute-start.2) | collective-permute-done | bytes 131104 | tf_op jit(solution)/shard_map/ppermute | solution.py:317
  42.0 1.7 %gram.1 = f32[192,512]{1,0:T(8,128)} custom-call(s32[4]{0:T(128)S(1)} %pad_add_fusion.w_ref, f32[64,512]{1,0:T(8,128)S(1)} %sum_parts.2.own_ref, f32[64,512]{1,0:T(8,128)S(1)} %collective-permute-done.2.oth_ref, f32[64,512]{1,0:T(8,128)S(1)} %panel_rows.1.after_ref.z_own_ref, f32[64,512]{1,0:T(8,128)S(1)} %collective-permute-done.3.z_oth_ref), custom_call_target="tpu_custom_call" | custom-call | tf_op jit(solution)/shard_map/gram/pallas_call | solution.py:319
  43.7 3.5 %all-to-all-start.2 = ((f32[8,24,512]{2,1,0:T(8,128)}), f32[8,24,512]{2,1,0:T(8,128)S(1)}, u32[]{:S(2)}, u32[]{:S(2)}) async-start(f32[8,24,512]{2,1,0:T(8,128)} %bitcast.11), calls=%async_computation.2 | async-start | bytes 786432 | tf_op jit(solution)/shard_map/all_to_all | solution.py:282
  47.2 0.0 copy-done
  47.2 0.0 copy-done.2
  47.2 2.1 %chunks.1 = (f32[512,512]{1,0:T(8,128)}, f32[256,256]{1,0:T(8,128)S(1)}, f32[256,256]{1,0:T(8,128)S(1)}) custom-call(s32[4]{0:T(128)S(1)} %pad_add_fusion.w_ref, f32[64,512]{1,0:T(8,128)S(1)} %sum_parts.2.own_ref, s32[1,48]{1,0:T(1,128)S(1)} %bitcast.23, s32[1,32]{1,0:T(1,128)S(1)} %bitcast.26, f32[256,256]{1,0:T(8,128)S(1)} %copy-done.1, ...), custom_call_target="tpu_custom_call" | custom-call | tf_op jit(solution)/shard_map/chunks/pallas_call | solution.py:330
  49.3 4.7 %all-to-all-done.2 = f32[8,24,512]{2,1,0:T(8,128)S(1)} async-done(((f32[8,24,512]{2,1,0:T(8,128)}), f32[8,24,512]{2,1,0:T(8,128)S(1)}, u32[]{:S(2)}, u32[]{:S(2)}) %all-to-all-start.2) | async-done | bytes 393248 | tf_op jit(solution)/shard_map/all_to_all | solution.py:282
  54.0 4.6 %all-to-all-start.1 = ((f32[8,64,512]{2,1,0:T(8,128)}), f32[8,64,512]{2,1,0:T(8,128)S(1)}, u32[]{:S(2)}, u32[]{:S(2)}) async-start(f32[8,64,512]{2,1,0:T(8,128)} %bitcast.9), calls=%async_computation.1 | async-start | bytes 2097152 | tf_op jit(solution)/shard_map/all_to_all | solution.py:282
  58.7 0.4 collective-permute-start.7
  59.1 0.1 collective-permute-start.6
  59.2 2.6 %collective-permute-start.5 = (f32[24,512]{1,0:T(8,128)S(1)}, f32[24,512]{1,0:T(8,128)S(1)}, u32[]{:S(2)}, u32[]{:S(2)}) collective-permute-start(f32[24,512]{1,0:T(8,128)S(1)} %sum_parts.3.own_ref), channel_id=1, source_target_pairs={{0,48},{16,0},{32,16},{48,32},{1,49},{17,1},{33,17},{49,33},{2,50}... | collective-permute-start | bytes 147464 | tf_op jit(solution)/shard_map/ppermute | solution.py:286
  61.8 1.5 %collective-permute-done.7.across_ref = f32[24,512]{1,0:T(8,128)S(1)} collective-permute-done((f32[24,512]{1,0:T(8,128)S(1)}, f32[24,512]{1,0:T(8,128)S(1)}, u32[]{:S(2)}, u32[]{:S(2)}) %collective-permute-start.7) | collective-permute-done | bytes 49184 | tf_op jit(solution)/shard_map/ppermute | solution.py:286
  63.3 0.5 collective-permute-done.6.ahead_ref
  63.8 0.0 collective-permute-done.5.behind_ref
  63.8 1.7 %collective-permute-start.10 = (f32[24,512]{1,0:T(8,128)S(1)}, f32[24,512]{1,0:T(8,128)S(1)}, u32[]{:S(2)}, u32[]{:S(2)}) collective-permute-start(f32[24,512]{1,0:T(8,128)S(1)} %ring_sum.1.own_ref), channel_id=1, source_target_pairs={{0,128},{64,192},{128,0},{192,64},{1,129},{65,193},{129,1},{193,65... | collective-permute-start | bytes 147464 | tf_op jit(solution)/shard_map/ppermute | solution.py:286
  65.4 0.4 collective-permute-start.9
  65.9 3.1 %collective-permute-start.8 = (f32[24,512]{1,0:T(8,128)S(1)}, f32[24,512]{1,0:T(8,128)S(1)}, u32[]{:S(2)}, u32[]{:S(2)}) collective-permute-start(f32[24,512]{1,0:T(8,128)S(1)} %ring_sum.1.own_ref), channel_id=1, source_target_pairs={{0,192},{64,0},{128,64},{192,128},{1,193},{65,1},{129,65},{193,129... | collective-permute-start | bytes 147464 | tf_op jit(solution)/shard_map/ppermute | solution.py:286
  69.0 2.8 %collective-permute-done.10.across_ref = f32[24,512]{1,0:T(8,128)S(1)} collective-permute-done((f32[24,512]{1,0:T(8,128)S(1)}, f32[24,512]{1,0:T(8,128)S(1)}, u32[]{:S(2)}, u32[]{:S(2)}) %collective-permute-start.10) | collective-permute-done | bytes 49184 | tf_op jit(solution)/shard_map/ppermute | solution.py:286
  71.8 1.1 %collective-permute-done.9.ahead_ref = f32[24,512]{1,0:T(8,128)S(1)} collective-permute-done((f32[24,512]{1,0:T(8,128)S(1)}, f32[24,512]{1,0:T(8,128)S(1)}, u32[]{:S(2)}, u32[]{:S(2)}) %collective-permute-start.9) | collective-permute-done | bytes 49184 | tf_op jit(solution)/shard_map/ppermute | solution.py:286
  73.0 0.0 collective-permute-done.8.behind_ref
  73.0 0.8 spread.1
  73.8 0.0 all-to-all-done.1
  73.8 4.9 %all-to-all-start.3 = ((f32[8,24,512]{2,1,0:T(8,128)}), f32[8,24,512]{2,1,0:T(8,128)S(1)}, u32[]{:S(2)}, u32[]{:S(2)}) async-start(f32[8,24,512]{2,1,0:T(8,128)} %bitcast.13), calls=%async_computation.3 | async-start | bytes 786432 | tf_op jit(solution)/shard_map/all_to_all | solution.py:282
  78.7 3.7 %collective-permute-start.4 = (f32[512,512]{1,0:T(8,128)S(1)}, f32[512,512]{1,0:T(8,128)S(1)}, u32[]{:S(2)}, u32[]{:S(2)}) collective-permute-start(f32[512,512]{1,0:T(8,128)S(1)} %bitcast.15), channel_id=1, source_target_pairs={{0,1},{1,0},{2,3},{3,2},{4,5},{5,4},{6,7},{7,6},{8,9},{9,8},{10,11... | collective-permute-start | bytes 3145736 | tf_op jit(solution)/shard_map/ppermute | solution.py:359
  82.4 2.9 %all-to-all-done.3 = f32[8,24,512]{2,1,0:T(8,128)S(1)} async-done(((f32[8,24,512]{2,1,0:T(8,128)}), f32[8,24,512]{2,1,0:T(8,128)S(1)}, u32[]{:S(2)}, u32[]{:S(2)}) %all-to-all-start.3) | async-done | bytes 393248 | tf_op jit(solution)/shard_map/all_to_all | solution.py:282
  85.3 4.9 %collective-permute-start.11 = (f32[192,512]{1,0:T(8,128)S(1)}, f32[192,512]{1,0:T(8,128)S(1)}, u32[]{:S(2)}, u32[]{:S(2)}) collective-permute-start(f32[192,512]{1,0:T(8,128)S(1)} %bitcast.18), channel_id=1, source_target_pairs={{0,1},{1,0},{2,3},{3,2},{4,5},{5,4},{6,7},{7,6},{8,9},{9,8},{10,11... | collective-permute-start | bytes 1179656 | tf_op jit(solution)/shard_map/ppermute | solution.py:360
  90.1 0.0 collective-permute-done.4.oth_ref
  90.1 2.0 %assemble.1 = (f32[1024,256]{1,0:T(8,128)}, f32[1024,256]{1,0:T(8,128)}) custom-call(s32[4]{0:T(128)S(1)} %pad_add_fusion.w_ref, f32[512,512]{1,0:T(8,128)S(1)} %bitcast.16, f32[512,512]{1,0:T(8,128)S(1)} %collective-permute-done.4.oth_ref), custom_call_target="tpu_custom_call" | custom-call | tf_op jit(solution)/shard_map/assemble/pallas_call | solution.py:352
  92.2 0.0 collective-permute-done.11.oth_ref
  92.2 1.5 %last.1 = (f32[256,256]{1,0:T(8,128)}, f32[256,256]{1,0:T(8,128)}, f32[256,256]{1,0:T(8,128)}) custom-call(s32[4]{0:T(128)S(1)} %pad_add_fusion.w_ref, f32[192,512]{1,0:T(8,128)S(1)} %bitcast.19, f32[192,512]{1,0:T(8,128)S(1)} %collective-permute-done.11.oth_ref, f32[256,256]{1,0:T(8,128)S(1)} %copy-done, f32[256,256]{1,0:T(8,128)S(1)} %get-tuple-element.35.it_ref, ...), custom_call_target="tpu_custom_call" | custom-call | tf_op jit(solution)/shard_map/last/pallas_call | solution.py:362
  (2 shorter events, 0.0 us)
Async XLA Ops:
  6.4 18.7 %collective-permute-start.1 = (f32[64,512]{1,0:T(8,128)S(1)}, f32[64,512]{1,0:T(8,128)S(1)}, u32[]{:S(2)}, u32[]{:S(2)}) collective-permute-start(f32[64,512]{1,0:T(8,128)S(1)} %get-tuple-element.27), channel_id=1, source_target_pairs={{0,15},{1,21},{2,45},{3,52},{4,71},{5,82},{6,97},{7,119},{8,133},{... | collective-permute-start | bytes 393224 | tf_op jit(solution)/shard_map/ppermute | solution.py:304
  11.1 2.8 %collective-permute-start = (f32[512,512]{1,0:T(8,128)S(1)}, f32[512,512]{1,0:T(8,128)S(1)}, u32[]{:S(2)}, u32[]{:S(2)}) collective-permute-start(f32[512,512]{1,0:T(8,128)S(1)} %get-tuple-element.26), channel_id=1, source_target_pairs={{0,1},{1,0},{2,3},{3,2},{4,5},{5,4},{6,7},{7,6},{8,9},{9,8},{10,11... | collective-permute-start | bytes 3145736 | tf_op jit(solution)/shard_map/ppermute | solution.py:141
  13.4 11.8 %copy-start.1 = (f32[256,256]{1,0:T(8,128)S(1)}, f32[256,256]{1,0:T(8,128)}, u32[]{:S(2)}) copy-start(f32[256,256]{1,0:T(8,128)} %top_ref.3) | copy-start | bytes 786436
  13.4 11.8 %copy-start.3 = (s32[48]{0:T(128)S(1)}, s32[48]{0:T(128)}, u32[]{:S(2)}) copy-start(s32[48]{0:T(128)} %param.12) | copy-start | bytes 580
  13.4 11.8 %copy-start.4 = (s32[32]{0:T(128)S(1)}, s32[32]{0:T(128)}, u32[]{:S(2)}) copy-start(s32[32]{0:T(128)} %param.13) | copy-start | bytes 388
  14.9 25.2 %all-to-all-start = ((f32[8,64,512]{2,1,0:T(8,128)}), f32[8,64,512]{2,1,0:T(8,128)S(1)}, u32[]{:S(2)}, u32[]{:S(2)}) async-start(f32[8,64,512]{2,1,0:T(8,128)} %bitcast.7), calls=%async_computation | async-start | bytes 2097152 | tf_op jit(solution)/shard_map/all_to_all | solution.py:282
  25.1 22.0 %copy-start = (f32[256,256]{1,0:T(8,128)S(1)}, f32[256,256]{1,0:T(8,128)}, u32[]{:S(2)}) copy-start(f32[256,256]{1,0:T(8,128)} %inv2_ref.3) | copy-start | bytes 786436
  25.2 22.0 %copy-start.2 = (f32[256,256]{1,0:T(8,128)S(1)}, f32[256,256]{1,0:T(8,128)}, u32[]{:S(2)}) copy-start(f32[256,256]{1,0:T(8,128)} %inv1_ref.1) | copy-start | bytes 786436
  26.0 15.0 %collective-permute-start.3 = (f32[64,512]{1,0:T(8,128)S(1)}, f32[64,512]{1,0:T(8,128)S(1)}, u32[]{:S(2)}, u32[]{:S(2)}) collective-permute-start(f32[64,512]{1,0:T(8,128)S(1)} %panel_rows.1.after_ref.z_own_ref), channel_id=1, source_target_pairs={{0,1},{1,0},{2,3},{3,2},{4,5},{5,4},{6,7},{7,6},{8,9},{9,8},{10,11... | collective-permute-start | bytes 393224 | tf_op jit(solution)/shard_map/ppermute | solution.py:315
  40.2 1.8 %collective-permute-start.2 = (f32[64,512]{1,0:T(8,128)S(1)}, f32[64,512]{1,0:T(8,128)S(1)}, u32[]{:S(2)}, u32[]{:S(2)}) collective-permute-start(f32[64,512]{1,0:T(8,128)S(1)} %sum_parts.2.own_ref), channel_id=1, source_target_pairs={{0,1},{1,0},{2,3},{3,2},{4,5},{5,4},{6,7},{7,6},{8,9},{9,8},{10,11... | collective-permute-start | bytes 393224 | tf_op jit(solution)/shard_map/ppermute | solution.py:317
  43.7 10.3 %all-to-all-start.2 = ((f32[8,24,512]{2,1,0:T(8,128)}), f32[8,24,512]{2,1,0:T(8,128)S(1)}, u32[]{:S(2)}, u32[]{:S(2)}) async-start(f32[8,24,512]{2,1,0:T(8,128)} %bitcast.11), calls=%async_computation.2 | async-start | bytes 786432 | tf_op jit(solution)/shard_map/all_to_all | solution.py:282
  54.0 19.7 %all-to-all-start.1 = ((f32[8,64,512]{2,1,0:T(8,128)}), f32[8,64,512]{2,1,0:T(8,128)S(1)}, u32[]{:S(2)}, u32[]{:S(2)}) async-start(f32[8,64,512]{2,1,0:T(8,128)} %bitcast.9), calls=%async_computation.1 | async-start | bytes 2097152 | tf_op jit(solution)/shard_map/all_to_all | solution.py:282
  58.7 4.6 %collective-permute-start.7 = (f32[24,512]{1,0:T(8,128)S(1)}, f32[24,512]{1,0:T(8,128)S(1)}, u32[]{:S(2)}, u32[]{:S(2)}) collective-permute-start(f32[24,512]{1,0:T(8,128)S(1)} %sum_parts.3.own_ref), channel_id=1, source_target_pairs={{0,32},{16,48},{32,0},{48,16},{1,33},{17,49},{33,1},{49,17},{2,34}... | collective-permute-start | bytes 147464 | tf_op jit(solution)/shard_map/ppermute | solution.py:286
  59.1 4.7 %collective-permute-start.6 = (f32[24,512]{1,0:T(8,128)S(1)}, f32[24,512]{1,0:T(8,128)S(1)}, u32[]{:S(2)}, u32[]{:S(2)}) collective-permute-start(f32[24,512]{1,0:T(8,128)S(1)} %sum_parts.3.own_ref), channel_id=1, source_target_pairs={{0,16},{16,32},{32,48},{48,0},{1,17},{17,33},{33,49},{49,1},{2,18}... | collective-permute-start | bytes 147464 | tf_op jit(solution)/shard_map/ppermute | solution.py:286
  59.2 4.6 %collective-permute-start.5 = (f32[24,512]{1,0:T(8,128)S(1)}, f32[24,512]{1,0:T(8,128)S(1)}, u32[]{:S(2)}, u32[]{:S(2)}) collective-permute-start(f32[24,512]{1,0:T(8,128)S(1)} %sum_parts.3.own_ref), channel_id=1, source_target_pairs={{0,48},{16,0},{32,16},{48,32},{1,49},{17,1},{33,17},{49,33},{2,50}... | collective-permute-start | bytes 147464 | tf_op jit(solution)/shard_map/ppermute | solution.py:286
  63.8 8.1 %collective-permute-start.10 = (f32[24,512]{1,0:T(8,128)S(1)}, f32[24,512]{1,0:T(8,128)S(1)}, u32[]{:S(2)}, u32[]{:S(2)}) collective-permute-start(f32[24,512]{1,0:T(8,128)S(1)} %ring_sum.1.own_ref), channel_id=1, source_target_pairs={{0,128},{64,192},{128,0},{192,64},{1,129},{65,193},{129,1},{193,65... | collective-permute-start | bytes 147464 | tf_op jit(solution)/shard_map/ppermute | solution.py:286
  65.4 7.5 %collective-permute-start.9 = (f32[24,512]{1,0:T(8,128)S(1)}, f32[24,512]{1,0:T(8,128)S(1)}, u32[]{:S(2)}, u32[]{:S(2)}) collective-permute-start(f32[24,512]{1,0:T(8,128)S(1)} %ring_sum.1.own_ref), channel_id=1, source_target_pairs={{0,64},{64,128},{128,192},{192,0},{1,65},{65,129},{129,193},{193,1... | collective-permute-start | bytes 147464 | tf_op jit(solution)/shard_map/ppermute | solution.py:286
  65.9 7.1 %collective-permute-start.8 = (f32[24,512]{1,0:T(8,128)S(1)}, f32[24,512]{1,0:T(8,128)S(1)}, u32[]{:S(2)}, u32[]{:S(2)}) collective-permute-start(f32[24,512]{1,0:T(8,128)S(1)} %ring_sum.1.own_ref), channel_id=1, source_target_pairs={{0,192},{64,0},{128,64},{192,128},{1,193},{65,1},{129,65},{193,129... | collective-permute-start | bytes 147464 | tf_op jit(solution)/shard_map/ppermute | solution.py:286
  73.8 11.5 %all-to-all-start.3 = ((f32[8,24,512]{2,1,0:T(8,128)}), f32[8,24,512]{2,1,0:T(8,128)S(1)}, u32[]{:S(2)}, u32[]{:S(2)}) async-start(f32[8,24,512]{2,1,0:T(8,128)} %bitcast.13), calls=%async_computation.3 | async-start | bytes 786432 | tf_op jit(solution)/shard_map/all_to_all | solution.py:282
  78.7 11.5 %collective-permute-start.4 = (f32[512,512]{1,0:T(8,128)S(1)}, f32[512,512]{1,0:T(8,128)S(1)}, u32[]{:S(2)}, u32[]{:S(2)}) collective-permute-start(f32[512,512]{1,0:T(8,128)S(1)} %bitcast.15), channel_id=1, source_target_pairs={{0,1},{1,0},{2,3},{3,2},{4,5},{5,4},{6,7},{7,6},{8,9},{9,8},{10,11... | collective-permute-start | bytes 3145736 | tf_op jit(solution)/shard_map/ppermute | solution.py:359
  85.3 6.9 %collective-permute-start.11 = (f32[192,512]{1,0:T(8,128)S(1)}, f32[192,512]{1,0:T(8,128)S(1)}, u32[]{:S(2)}, u32[]{:S(2)}) collective-permute-start(f32[192,512]{1,0:T(8,128)S(1)} %bitcast.18), channel_id=1, source_target_pairs={{0,1},{1,0},{2,3},{3,2},{4,5},{5,4},{6,7},{7,6},{8,9},{9,8},{10,11... | collective-permute-start | bytes 1179656 | tf_op jit(solution)/shard_map/ppermute | solution.py:360

commit v2 on v1

--- a/solution.py
+++ b/solution.py
@@ -23,11 +23,13 @@
 MM = ((1,), (0,))
 TM = ((0,), (0,))
 ROUTE = (
-    0xCADEB16F, 0x52740983, 0xAEDC7695, 0x2F14803B, 0xBEF8C16D, 0x79A50432, 0x8EB91254, 0x3706FDAC,
-    0x0218FDE7, 0x6453AC9B, 0x64315072, 0xDF8AEB9C, 0x29FB0341, 0xC567AED8, 0xC2513467, 0x08E9FDBA,
-    0x43671025, 0xAE89CFDB, 0x46731052, 0x9AEFBC8D, 0x47561302, 0x98EDAFBC, 0x36407125, 0xCA9BFE8D,
-    0x2430DEA1, 0xBC98F756, 0x421DBC8F, 0x5E9A3076, 0x0347E9AF, 0xD8CB5261, 0x6570F8DA, 0xB9CE2413,
+    0xBFDC2745, 0x0163E98A, 0xFCDB3245, 0x10769EA8, 0xEFD96704, 0x51328CBA, 0xEF897614, 0x0325CABD,
+    0x26104573, 0xFDCB9AE8, 0x30175264, 0xCDEFAB98, 0x42310576, 0xC9EF8BAD, 0x30124765, 0x98FEABCD,
+    0x52641073, 0xB89FAEDC, 0x27450631, 0x98EABFDC, 0x76501432, 0xCDBAFE89, 0x76410532, 0xDAB9FC8E,
+    0x3457BCDA, 0x8EF90621, 0x4536DCBF, 0xEA982710, 0x6057FCDE, 0xAB892314, 0x45679EF8, 0xABDC2310,
 )
+Y_ORDER = (2, 1, 3)
+Z_ORDER = (1, 3, 2)
 SWAP = [(0, 1), (1, 0)]
 VM = pl.BlockSpec(memory_space=pltpu.VMEM)
 SM = pl.BlockSpec(memory_space=pltpu.SMEM)
@@ -57,9 +59,8 @@
     return jnp.max(jnp.where(listed == block, 1.0, 0.0), axis=1, keepdims=True)
 
 
-def product_rows(s_ref, low, high, z, p_ref):
-    rows = split(s_ref[pl.ds(low, high - low)].reshape((high - low) * CH, ROWS))
-    p_ref[pl.ds(low * CH, (high - low) * CH), :] = dot3(rows, z, MM)
+def product_rows(s_ref, low, high, z):
+    return dot3(split(s_ref[pl.ds(low, high - low)].reshape((high - low) * CH, ROWS)), z, MM)
 
 
 def send_kernel(w_ref, s_hbm, two_hbm, one_hbm, top_hbm, b2_hbm, b1_hbm, p_ref, zh_ref, zl_ref, keep_ref, part_ref,
@@ -103,15 +104,17 @@
     z = (zh_ref[...], zl_ref[...])
     for i in range(STEPS):
         copies[3 + 2 * blocks + i].wait()
-        product_rows(s_ref, i * per, (i + 1) * per, z, p_ref)
+        p_ref[pl.ds(i * per * CH, per * CH), :] = product_rows(s_ref, i * per, (i + 1) * per, z)
     for copy in copies[3 + 2 * blocks + STEPS:]:
         copy.wait()
 
 
-def keep_kernel(s_ref, zh_ref, zl_ref, p_ref):
+def keep_kernel(s_ref, zh_ref, zl_ref, got_ref, p_ref):
+    per = CHIPS // STEPS
     z = (zh_ref[...], zl_ref[...])
     for i in range(STEPS):
-        product_rows(s_ref, i * CHIPS // STEPS, (i + 1) * CHIPS // STEPS, z, p_ref)
+        rows = pl.ds(i * per * CH, per * CH)
+        p_ref[rows, :] = got_ref[rows, :] + product_rows(s_ref, i * per, (i + 1) * per, z)
 
 
 def products(where, sigma, two, one, top, b2, b1):
@@ -139,18 +142,15 @@
     )(where, *map(in_hbm, (sigma, two, one, top, b2, b1)))
 
     got = lax.ppermute(send, "c", SWAP)
-    keep = pl.pallas_call(
+    pair = pl.pallas_call(
         keep_kernel,
-        in_specs=[VM] * 3,
+        in_specs=[VM] * 4,
         out_specs=VM,
         out_shape=shape_p,
         compiler_params=PARAMS,
         cost_estimate=LONG,
         name="product_keep",
-    )(mine, zh, zl)
-    pair = pl.pallas_call(
-        add_kernel, in_specs=[VM] * 2, out_specs=VM, out_shape=shape_p, compiler_params=PARAMS, name="pair_sum"
-    )(keep, got)
+    )(mine, zh, zl, got)
     return pair, part
 
 
@@ -174,12 +174,13 @@
     )(value, after)
 
 
-def ring_kernel(own_ref, behind_ref, ahead_ref, across_ref, out_ref):
-    out_ref[...] = (own_ref[...] + across_ref[...]) + (ahead_ref[...] + behind_ref[...])
-
-
-def add_kernel(left_ref, right_ref, out_ref):
-    out_ref[...] = left_ref[...] + right_ref[...]
+def ring_total(order, refs):
+    by = dict(zip(order, refs[1:]))
+    return (refs[0][...] + by[2][...]) + (by[1][...] + by[3][...])
+
+
+def ring_kernel(order, *refs):
+    refs[4][...] = ring_total(order, refs)
 
 
 def chunk_kernel(w_ref, own_ref, b2_ref, b1_ref, top_ref, inv2_ref, inv1_ref, chunk_ref, it_ref, base_ref):
@@ -195,10 +196,10 @@
     base_ref[...] = inv1_ref[...] + dot3(top, split(it), TM)
 
 
-def spread_kernel(own_ref, behind_ref, ahead_ref, across_ref, out_ref):
-    total = (own_ref[...] + across_ref[...]) + (ahead_ref[...] + behind_ref[...])
+def spread_kernel(order, *refs):
+    total = ring_total(order, refs)
     for q in range(CHIPS):
-        out_ref[pl.ds(q * GR, GR), :] = total
+        refs[4][pl.ds(q * GR, GR), :] = total
 
 
 def rows_kernel(w_ref, z_ref, top_ref, b2_ref, b1_ref, live_ref):
@@ -282,9 +283,8 @@
     return lax.all_to_all(value, axes, 0, 0, tiled=True)
 
 
-def ring(value, axis):
-    shift = lambda k: lax.ppermute(value, axis, [(i, (i + k) % 4) for i in range(4)])
-    return value, shift(3), shift(1), shift(2)
+def ring(value, axis, order):
+    return [value] + [lax.ppermute(value, axis, [(i, (i + k) % 4) for i in range(4)]) for k in order]
 
 
 def per_device(sigma, two, one, top, blocks_two, blocks_one, inv2, inv1):
@@ -339,12 +339,12 @@
 
     g = sum_parts(g, base)
     g = pl.pallas_call(
-        ring_kernel, in_specs=[VM] * 4, out_specs=VM, out_shape=jax.ShapeDtypeStruct((GR, W), F32),
+        functools.partial(ring_kernel, Y_ORDER), in_specs=[VM] * 4, out_specs=VM, out_shape=jax.ShapeDtypeStruct((GR, W), F32),
         compiler_params=PARAMS, name="ring_sum",
-    )(*ring(g, "y"))
-    g = ring(g, "zh")
+    )(*ring(g, "y", Y_ORDER))
+    g = ring(g, "zh", Z_ORDER)
     g = pl.pallas_call(
-        spread_kernel, in_specs=[VM] * 4, out_specs=VM, out_shape=parts, compiler_params=PARAMS, name="spread"
+        functools.partial(spread_kernel, Z_ORDER), in_specs=[VM] * 4, out_specs=VM, out_shape=parts, compiler_params=PARAMS, name="spread"
     )(*g)
     g = a2a(g, ("zl", "x"))
 

time: 94.1 us -> 93.4 us (level)
  waiting for transfers between devices: 28.6 us -> 26.9 us
  starting transfers between devices: 46.6 us -> 47.7 us
    ppermute x1, starting transfers between devices: 0.47 us -> 3.32 us  [products(): got = lax.ppermute(send, 'c', SWAP)]
    ppermute x1, starting transfers between devices: 4.67 us -> 2.02 us  [per_device(): z_own = lax.ppermute(part, AXES, turn)]
    ppermute x6, starting transfers between devices: 8.32 us -> 10.9 us  [ring(): lax.ppermute(value, axis, [(i, (i + k) % 4) for i in range(4)])]
    ppermute x6, waiting for transfers between devices: 5.94 us -> 4.24 us  [ring(): lax.ppermute(value, axis, [(i, (i + k) % 4) for i in range(4)])]
    pallas_call x4 -> x3, Pallas kernels: 3.66 us -> 3.62 us  [the longest x1 2.83 us: products(): pl.pallas_call(keep_kernel, in_specs=[VM] * 4, out_specs=VM, out_shape=sh...]
where the time goes in v2:
time: 93.4 us; the launch traced here: 93 us
  starting transfers between devices  47.7 us (51%)
  waiting for transfers between devices  26.9 us (29%)
  Pallas kernels  17.4 us (19%)
    all_to_all x4, starting transfers between devices, a2a(): return lax.all_to_all(value, axes, 0, 0, tiled=True)  22.6 us
    all_to_all x4, waiting for transfers between devices, a2a(): return lax.all_to_all(value, axes, 0, 0, tiled=True)  21.4 us
    ppermute x6, starting transfers between devices, ring(): lax.ppermute(value, axis, [(i, (i + k) % 4) for i in range(4)])  10.9 us
    pallas_call x1, Pallas kernels, products(): pl.pallas_call(send_kernel, in_specs=[SM] + [HBM] * 6, out_specs=[VM] * 5...  5.55 us
    ppermute x6, waiting for transfers between devices, ring(): lax.ppermute(value, axis, [(i, (i + k) % 4) for i in range(4)])  4.24 us
    ppermute x1, starting transfers between devices, per_device(): g_oth = lax.ppermute(g, 'c', SWAP)  4.02 us
    ppermute x1, starting transfers between devices, products(): got = lax.ppermute(send, 'c', SWAP)  3.32 us
    ppermute x1, starting transfers between devices, per_device(): lax.ppermute(chunks, 'c', SWAP)  2.87 us
  transfers between devices with their start and end apart: 16, of which 9 were waited for; matrix products, arithmetic and copies ran while one was open for 0% of the time, Pallas kernels for 9%

profile of v2, /device:TPU:1, one launch (start us, length us, event | category | flops | bytes accessed | tf_op | source)
XLA Modules:
  0.0 93.0 jit_solution(8356420899620070001)
XLA Ops:
  0.8 0.1 pad_add_fusion.w_ref
  0.9 5.6 %product_send.1 = (f32[512,512]{1,0:T(8,128)S(1)}, bf16[1024,512]{1,0:T(8,128)(2,1)S(1)}, bf16[1024,512]{1,0:T(8,128)(2,1)S(1)}, f32[8,64,1024]{2,1,0:T(8,128)S(1)}, f32[64,512]{1,0:T(8,128)S(1)}) custom-call(s32[4]{0:T(128)S(1)} %pad_add_fusion.w_ref, f32[8,128,1024]{2,1,0:T(8,128)} %bitcast.27, f32[1024,256]{1,0:T(8,128)} %two_hbm.1, f32[1024,256]{1,0:T(8,128)} %one_hbm.1, ...), custom_call_target="tpu_custom_call" | custom-call | flops 21474836480 | bytes 8388608 | tf_op jit(solution)/shard_map/product_send/pallas_call | solution.py:125
  6.4 3.3 %collective-permute-start = (f32[512,512]{1,0:T(8,128)S(1)}, f32[512,512]{1,0:T(8,128)S(1)}, u32[]{:S(2)}, u32[]{:S(2)}) collective-permute-start(f32[512,512]{1,0:T(8,128)S(1)} %get-tuple-element.26), channel_id=1, source_target_pairs={{0,1},{1,0},{2,3},{3,2},{4,5},{5,4},{6,7},{7,6},{8,9},{9,8},{10,11... | collective-permute-start | bytes 3145736 | tf_op jit(solution)/shard_map/ppermute | solution.py:144
  9.7 2.0 %collective-permute-start.1 = (f32[64,512]{1,0:T(8,128)S(1)}, f32[64,512]{1,0:T(8,128)S(1)}, u32[]{:S(2)}, u32[]{:S(2)}) collective-permute-start(f32[64,512]{1,0:T(8,128)S(1)} %get-tuple-element.27), channel_id=1, source_target_pairs={{0,5},{1,21},{2,36},{3,52},{4,67},{5,84},{6,102},{7,117},{8,131},{... | collective-permute-start | bytes 393224 | tf_op jit(solution)/shard_map/ppermute | solution.py:304
  11.8 0.3 collective-permute-done.got_ref
  12.0 0.0 copy-start.1
  12.0 0.0 copy-start.3
  12.0 0.0 copy-start.4
  12.0 2.8 %product_keep.1 = f32[512,512]{1,0:T(8,128)} custom-call(f32[8,64,1024]{2,1,0:T(8,128)S(1)} %get-tuple-element.23.s_ref, bf16[1024,512]{1,0:T(8,128)(2,1)S(1)} %get-tuple-element.24.zh_ref, bf16[1024,512]{1,0:T(8,128)(2,1)S(1)} %get-tuple-element.25.zl_ref, f32[512,512]{1,0:T(8,128)S(1)} %collective-permute-done.got_ref), custom_call_target="tpu_custom_call" | custom-call | flops 21474836480 | bytes 8388608 | tf_op jit(solution)/shard_map/product_keep/pallas_call | solution.py:145
  14.9 8.6 %all-to-all-start = ((f32[8,64,512]{2,1,0:T(8,128)}), f32[8,64,512]{2,1,0:T(8,128)S(1)}, u32[]{:S(2)}, u32[]{:S(2)}) async-start(f32[8,64,512]{2,1,0:T(8,128)} %bitcast.7), calls=%async_computation | async-start | bytes 2097152 | tf_op jit(solution)/shard_map/all_to_all | solution.py:283
  23.4 0.0 copy-start
  23.4 0.0 copy-start.2
  23.5 0.0 collective-permute-done.1.z_ref
  23.5 0.0 copy-done.1
  23.5 0.0 copy-done.3
  23.5 0.0 copy-done.4
  23.5 0.8 panel_rows.1.after_ref.z_own_ref
  24.3 1.0 %collective-permute-start.3 = (f32[64,512]{1,0:T(8,128)S(1)}, f32[64,512]{1,0:T(8,128)S(1)}, u32[]{:S(2)}, u32[]{:S(2)}) collective-permute-start(f32[64,512]{1,0:T(8,128)S(1)} %panel_rows.1.after_ref.z_own_ref), channel_id=1, source_target_pairs={{0,1},{1,0},{2,3},{3,2},{4,5},{5,4},{6,7},{7,6},{8,9},{9,8},{10,11... | collective-permute-start | bytes 393224 | tf_op jit(solution)/shard_map/ppermute | solution.py:315
  25.3 13.0 %all-to-all-done = f32[8,64,512]{2,1,0:T(8,128)S(1)} async-done(((f32[8,64,512]{2,1,0:T(8,128)}), f32[8,64,512]{2,1,0:T(8,128)S(1)}, u32[]{:S(2)}, u32[]{:S(2)}) %all-to-all-start) | async-done | bytes 1048608 | tf_op jit(solution)/shard_map/all_to_all | solution.py:283
  38.3 0.1 sum_parts.2.own_ref
  38.4 0.9 %collective-permute-start.2 = (f32[64,512]{1,0:T(8,128)S(1)}, f32[64,512]{1,0:T(8,128)S(1)}, u32[]{:S(2)}, u32[]{:S(2)}) collective-permute-start(f32[64,512]{1,0:T(8,128)S(1)} %sum_parts.2.own_ref), channel_id=1, source_target_pairs={{0,1},{1,0},{2,3},{3,2},{4,5},{5,4},{6,7},{7,6},{8,9},{9,8},{10,11... | collective-permute-start | bytes 393224 | tf_op jit(solution)/shard_map/ppermute | solution.py:317
  39.3 0.0 collective-permute-done.3.z_oth_ref
  39.3 1.0 %collective-permute-done.2.oth_ref = f32[64,512]{1,0:T(8,128)S(1)} collective-permute-done((f32[64,512]{1,0:T(8,128)S(1)}, f32[64,512]{1,0:T(8,128)S(1)}, u32[]{:S(2)}, u32[]{:S(2)}) %collective-permute-start.2) | collective-permute-done | bytes 131104 | tf_op jit(solution)/shard_map/ppermute | solution.py:317
  40.3 1.7 %gram.1 = f32[192,512]{1,0:T(8,128)} custom-call(s32[4]{0:T(128)S(1)} %pad_add_fusion.w_ref, f32[64,512]{1,0:T(8,128)S(1)} %sum_parts.2.own_ref, f32[64,512]{1,0:T(8,128)S(1)} %collective-permute-done.2.oth_ref, f32[64,512]{1,0:T(8,128)S(1)} %panel_rows.1.after_ref.z_own_ref, f32[64,512]{1,0:T(8,128)S(1)} %collective-permute-done.3.z_oth_ref), custom_call_target="tpu_custom_call" | custom-call | tf_op jit(solution)/shard_map/gram/pallas_call | solution.py:319
  42.0 3.5 %all-to-all-start.2 = ((f32[8,24,512]{2,1,0:T(8,128)}), f32[8,24,512]{2,1,0:T(8,128)S(1)}, u32[]{:S(2)}, u32[]{:S(2)}) async-start(f32[8,24,512]{2,1,0:T(8,128)} %bitcast.11), calls=%async_computation.2 | async-start | bytes 786432 | tf_op jit(solution)/shard_map/all_to_all | solution.py:283
  45.5 0.0 copy-done
  45.5 0.0 copy-done.2
  45.5 2.1 %chunks.1 = (f32[512,512]{1,0:T(8,128)}, f32[256,256]{1,0:T(8,128)S(1)}, f32[256,256]{1,0:T(8,128)S(1)}) custom-call(s32[4]{0:T(128)S(1)} %pad_add_fusion.w_ref, f32[64,512]{1,0:T(8,128)S(1)} %sum_parts.2.own_ref, s32[1,48]{1,0:T(1,128)S(1)} %bitcast.23, s32[1,32]{1,0:T(1,128)S(1)} %bitcast.26, f32[256,256]{1,0:T(8,128)S(1)} %copy-done.1, ...), custom_call_target="tpu_custom_call" | custom-call | tf_op jit(solution)/shard_map/chunks/pallas_call | solution.py:330
  47.6 4.7 %all-to-all-done.2 = f32[8,24,512]{2,1,0:T(8,128)S(1)} async-done(((f32[8,24,512]{2,1,0:T(8,128)}), f32[8,24,512]{2,1,0:T(8,128)S(1)}, u32[]{:S(2)}, u32[]{:S(2)}) %all-to-all-start.2) | async-done | bytes 393248 | tf_op jit(solution)/shard_map/all_to_all | solution.py:283
  52.3 4.6 %all-to-all-start.1 = ((f32[8,64,512]{2,1,0:T(8,128)}), f32[8,64,512]{2,1,0:T(8,128)S(1)}, u32[]{:S(2)}, u32[]{:S(2)}) async-start(f32[8,64,512]{2,1,0:T(8,128)} %bitcast.9), calls=%async_computation.1 | async-start | bytes 2097152 | tf_op jit(solution)/shard_map/all_to_all | solution.py:283
  57.0 1.5 %collective-permute-start.5 = (f32[24,512]{1,0:T(8,128)S(1)}, f32[24,512]{1,0:T(8,128)S(1)}, u32[]{:S(2)}, u32[]{:S(2)}) collective-permute-start(f32[24,512]{1,0:T(8,128)S(1)} %sum_parts.3.refs_0_), channel_id=1, source_target_pairs={{0,32},{16,48},{32,0},{48,16},{1,33},{17,49},{33,1},{49,17},{2,34}... | collective-permute-start | bytes 147464 | tf_op jit(solution)/shard_map/ppermute | solution.py:287
  58.5 0.5 collective-permute-start.6
  59.0 2.2 %collective-permute-start.7 = (f32[24,512]{1,0:T(8,128)S(1)}, f32[24,512]{1,0:T(8,128)S(1)}, u32[]{:S(2)}, u32[]{:S(2)}) collective-permute-start(f32[24,512]{1,0:T(8,128)S(1)} %sum_parts.3.refs_0_), channel_id=1, source_target_pairs={{0,48},{16,0},{32,16},{48,32},{1,49},{17,1},{33,17},{49,33},{2,50}... | collective-permute-start | bytes 147464 | tf_op jit(solution)/shard_map/ppermute | solution.py:287
  61.2 0.4 collective-permute-done.5.refs_1_
  61.5 1.3 %collective-permute-done.6.refs_2_ = f32[24,512]{1,0:T(8,128)S(1)} collective-permute-done((f32[24,512]{1,0:T(8,128)S(1)}, f32[24,512]{1,0:T(8,128)S(1)}, u32[]{:S(2)}, u32[]{:S(2)}) %collective-permute-start.6) | collective-permute-done | bytes 49184 | tf_op jit(solution)/shard_map/ppermute | solution.py:287
  62.8 0.0 collective-permute-done.7.refs_3_
  62.8 3.1 %collective-permute-start.10 = (f32[24,512]{1,0:T(8,128)S(1)}, f32[24,512]{1,0:T(8,128)S(1)}, u32[]{:S(2)}, u32[]{:S(2)}) collective-permute-start(f32[24,512]{1,0:T(8,128)S(1)} %ring_sum.1.refs_0_), channel_id=1, source_target_pairs={{0,128},{64,192},{128,0},{192,64},{1,129},{65,193},{129,1},{193,65... | collective-permute-start | bytes 147464 | tf_op jit(solution)/shard_map/ppermute | solution.py:287
  65.9 1.2 %collective-permute-start.8 = (f32[24,512]{1,0:T(8,128)S(1)}, f32[24,512]{1,0:T(8,128)S(1)}, u32[]{:S(2)}, u32[]{:S(2)}) collective-permute-start(f32[24,512]{1,0:T(8,128)S(1)} %ring_sum.1.refs_0_), channel_id=1, source_target_pairs={{0,64},{64,128},{128,192},{192,0},{1,65},{65,129},{129,193},{193,1... | collective-permute-start | bytes 147464 | tf_op jit(solution)/shard_map/ppermute | solution.py:287
  67.1 2.4 %collective-permute-start.9 = (f32[24,512]{1,0:T(8,128)S(1)}, f32[24,512]{1,0:T(8,128)S(1)}, u32[]{:S(2)}, u32[]{:S(2)}) collective-permute-start(f32[24,512]{1,0:T(8,128)S(1)} %ring_sum.1.refs_0_), channel_id=1, source_target_pairs={{0,192},{64,0},{128,64},{192,128},{1,193},{65,1},{129,65},{193,129... | collective-permute-start | bytes 147464 | tf_op jit(solution)/shard_map/ppermute | solution.py:287
  69.5 1.0 %collective-permute-done.10.refs_3_ = f32[24,512]{1,0:T(8,128)S(1)} collective-permute-done((f32[24,512]{1,0:T(8,128)S(1)}, f32[24,512]{1,0:T(8,128)S(1)}, u32[]{:S(2)}, u32[]{:S(2)}) %collective-permute-start.10) | collective-permute-done | bytes 49184 | tf_op jit(solution)/shard_map/ppermute | solution.py:287
  70.6 1.6 %collective-permute-done.8.refs_1_ = f32[24,512]{1,0:T(8,128)S(1)} collective-permute-done((f32[24,512]{1,0:T(8,128)S(1)}, f32[24,512]{1,0:T(8,128)S(1)}, u32[]{:S(2)}, u32[]{:S(2)}) %collective-permute-start.8) | collective-permute-done | bytes 49184 | tf_op jit(solution)/shard_map/ppermute | solution.py:287
  72.1 0.0 collective-permute-done.9.refs_2_
  72.2 0.8 spread.1
  72.9 0.0 all-to-all-done.1
  72.9 5.9 %all-to-all-start.3 = ((f32[8,24,512]{2,1,0:T(8,128)}), f32[8,24,512]{2,1,0:T(8,128)S(1)}, u32[]{:S(2)}, u32[]{:S(2)}) async-start(f32[8,24,512]{2,1,0:T(8,128)} %bitcast.13), calls=%async_computation.3 | async-start | bytes 786432 | tf_op jit(solution)/shard_map/all_to_all | solution.py:283
  78.8 2.9 %collective-permute-start.4 = (f32[512,512]{1,0:T(8,128)S(1)}, f32[512,512]{1,0:T(8,128)S(1)}, u32[]{:S(2)}, u32[]{:S(2)}) collective-permute-start(f32[512,512]{1,0:T(8,128)S(1)} %bitcast.15), channel_id=1, source_target_pairs={{0,1},{1,0},{2,3},{3,2},{4,5},{5,4},{6,7},{7,6},{8,9},{9,8},{10,11... | collective-permute-start | bytes 3145736 | tf_op jit(solution)/shard_map/ppermute | solution.py:359
  81.7 3.7 %all-to-all-done.3 = f32[8,24,512]{2,1,0:T(8,128)S(1)} async-done(((f32[8,24,512]{2,1,0:T(8,128)}), f32[8,24,512]{2,1,0:T(8,128)S(1)}, u32[]{:S(2)}, u32[]{:S(2)}) %all-to-all-start.3) | async-done | bytes 393248 | tf_op jit(solution)/shard_map/all_to_all | solution.py:283
  85.4 4.0 %collective-permute-start.11 = (f32[192,512]{1,0:T(8,128)S(1)}, f32[192,512]{1,0:T(8,128)S(1)}, u32[]{:S(2)}, u32[]{:S(2)}) collective-permute-start(f32[192,512]{1,0:T(8,128)S(1)} %bitcast.18), channel_id=1, source_target_pairs={{0,1},{1,0},{2,3},{3,2},{4,5},{5,4},{6,7},{7,6},{8,9},{9,8},{10,11... | collective-permute-start | bytes 1179656 | tf_op jit(solution)/shard_map/ppermute | solution.py:360
  89.5 0.0 collective-permute-done.4.oth_ref
  89.5 2.0 %assemble.1 = (f32[1024,256]{1,0:T(8,128)}, f32[1024,256]{1,0:T(8,128)}) custom-call(s32[4]{0:T(128)S(1)} %pad_add_fusion.w_ref, f32[512,512]{1,0:T(8,128)S(1)} %bitcast.16, f32[512,512]{1,0:T(8,128)S(1)} %collective-permute-done.4.oth_ref), custom_call_target="tpu_custom_call" | custom-call | tf_op jit(solution)/shard_map/assemble/pallas_call | solution.py:352
  91.5 0.0 collective-permute-done.11.oth_ref
  91.5 1.5 %last.1 = (f32[256,256]{1,0:T(8,128)}, f32[256,256]{1,0:T(8,128)}, f32[256,256]{1,0:T(8,128)}) custom-call(s32[4]{0:T(128)S(1)} %pad_add_fusion.w_ref, f32[192,512]{1,0:T(8,128)S(1)} %bitcast.19, f32[192,512]{1,0:T(8,128)S(1)} %collective-permute-done.11.oth_ref, f32[256,256]{1,0:T(8,128)S(1)} %copy-done, f32[256,256]{1,0:T(8,128)S(1)} %get-tuple-element.35.it_ref, ...), custom_call_target="tpu_custom_call" | custom-call | tf_op jit(solution)/shard_map/last/pallas_call | solution.py:362
  (2 shorter events, 0.0 us)
Async XLA Ops:
  6.4 5.6 %collective-permute-start = (f32[512,512]{1,0:T(8,128)S(1)}, f32[512,512]{1,0:T(8,128)S(1)}, u32[]{:S(2)}, u32[]{:S(2)}) collective-permute-start(f32[512,512]{1,0:T(8,128)S(1)} %get-tuple-element.26), channel_id=1, source_target_pairs={{0,1},{1,0},{2,3},{3,2},{4,5},{5,4},{6,7},{7,6},{8,9},{9,8},{10,11... | collective-permute-start | bytes 3145736 | tf_op jit(solution)/shard_map/ppermute | solution.py:144
  9.7 13.7 %collective-permute-start.1 = (f32[64,512]{1,0:T(8,128)S(1)}, f32[64,512]{1,0:T(8,128)S(1)}, u32[]{:S(2)}, u32[]{:S(2)}) collective-permute-start(f32[64,512]{1,0:T(8,128)S(1)} %get-tuple-element.27), channel_id=1, source_target_pairs={{0,5},{1,21},{2,36},{3,52},{4,67},{5,84},{6,102},{7,117},{8,131},{... | collective-permute-start | bytes 393224 | tf_op jit(solution)/shard_map/ppermute | solution.py:304
  12.0 11.4 %copy-start.1 = (f32[256,256]{1,0:T(8,128)S(1)}, f32[256,256]{1,0:T(8,128)}, u32[]{:S(2)}) copy-start(f32[256,256]{1,0:T(8,128)} %top_ref.3) | copy-start | bytes 786436
  12.0 11.4 %copy-start.3 = (s32[48]{0:T(128)S(1)}, s32[48]{0:T(128)}, u32[]{:S(2)}) copy-start(s32[48]{0:T(128)} %param.12) | copy-start | bytes 580
  12.0 11.5 %copy-start.4 = (s32[32]{0:T(128)S(1)}, s32[32]{0:T(128)}, u32[]{:S(2)}) copy-start(s32[32]{0:T(128)} %param.13) | copy-start | bytes 388
  14.9 23.5 %all-to-all-start = ((f32[8,64,512]{2,1,0:T(8,128)}), f32[8,64,512]{2,1,0:T(8,128)S(1)}, u32[]{:S(2)}, u32[]{:S(2)}) async-start(f32[8,64,512]{2,1,0:T(8,128)} %bitcast.7), calls=%async_computation | async-start | bytes 2097152 | tf_op jit(solution)/shard_map/all_to_all | solution.py:283
  23.4 22.0 %copy-start = (f32[256,256]{1,0:T(8,128)S(1)}, f32[256,256]{1,0:T(8,128)}, u32[]{:S(2)}) copy-start(f32[256,256]{1,0:T(8,128)} %inv2_ref.3) | copy-start | bytes 786436
  23.4 22.0 %copy-start.2 = (f32[256,256]{1,0:T(8,128)S(1)}, f32[256,256]{1,0:T(8,128)}, u32[]{:S(2)}) copy-start(f32[256,256]{1,0:T(8,128)} %inv1_ref.1) | copy-start | bytes 786436
  24.3 15.0 %collective-permute-start.3 = (f32[64,512]{1,0:T(8,128)S(1)}, f32[64,512]{1,0:T(8,128)S(1)}, u32[]{:S(2)}, u32[]{:S(2)}) collective-permute-start(f32[64,512]{1,0:T(8,128)S(1)} %panel_rows.1.after_ref.z_own_ref), channel_id=1, source_target_pairs={{0,1},{1,0},{2,3},{3,2},{4,5},{5,4},{6,7},{7,6},{8,9},{9,8},{10,11... | collective-permute-start | bytes 393224 | tf_op jit(solution)/shard_map/ppermute | solution.py:315
  38.4 1.9 %collective-permute-start.2 = (f32[64,512]{1,0:T(8,128)S(1)}, f32[64,512]{1,0:T(8,128)S(1)}, u32[]{:S(2)}, u32[]{:S(2)}) collective-permute-start(f32[64,512]{1,0:T(8,128)S(1)} %sum_parts.2.own_ref), channel_id=1, source_target_pairs={{0,1},{1,0},{2,3},{3,2},{4,5},{5,4},{6,7},{7,6},{8,9},{9,8},{10,11... | collective-permute-start | bytes 393224 | tf_op jit(solution)/shard_map/ppermute | solution.py:317
  42.0 10.3 %all-to-all-start.2 = ((f32[8,24,512]{2,1,0:T(8,128)}), f32[8,24,512]{2,1,0:T(8,128)S(1)}, u32[]{:S(2)}, u32[]{:S(2)}) async-start(f32[8,24,512]{2,1,0:T(8,128)} %bitcast.11), calls=%async_computation.2 | async-start | bytes 786432 | tf_op jit(solution)/shard_map/all_to_all | solution.py:283
  52.3 20.6 %all-to-all-start.1 = ((f32[8,64,512]{2,1,0:T(8,128)}), f32[8,64,512]{2,1,0:T(8,128)S(1)}, u32[]{:S(2)}, u32[]{:S(2)}) async-start(f32[8,64,512]{2,1,0:T(8,128)} %bitcast.9), calls=%async_computation.1 | async-start | bytes 2097152 | tf_op jit(solution)/shard_map/all_to_all | solution.py:283
  57.0 4.5 %collective-permute-start.5 = (f32[24,512]{1,0:T(8,128)S(1)}, f32[24,512]{1,0:T(8,128)S(1)}, u32[]{:S(2)}, u32[]{:S(2)}) collective-permute-start(f32[24,512]{1,0:T(8,128)S(1)} %sum_parts.3.refs_0_), channel_id=1, source_target_pairs={{0,32},{16,48},{32,0},{48,16},{1,33},{17,49},{33,1},{49,17},{2,34}... | collective-permute-start | bytes 147464 | tf_op jit(solution)/shard_map/ppermute | solution.py:287
  58.5 4.3 %collective-permute-start.6 = (f32[24,512]{1,0:T(8,128)S(1)}, f32[24,512]{1,0:T(8,128)S(1)}, u32[]{:S(2)}, u32[]{:S(2)}) collective-permute-start(f32[24,512]{1,0:T(8,128)S(1)} %sum_parts.3.refs_0_), channel_id=1, source_target_pairs={{0,16},{16,32},{32,48},{48,0},{1,17},{17,33},{33,49},{49,1},{2,18}... | collective-permute-start | bytes 147464 | tf_op jit(solution)/shard_map/ppermute | solution.py:287
  59.0 3.8 %collective-permute-start.7 = (f32[24,512]{1,0:T(8,128)S(1)}, f32[24,512]{1,0:T(8,128)S(1)}, u32[]{:S(2)}, u32[]{:S(2)}) collective-permute-start(f32[24,512]{1,0:T(8,128)S(1)} %sum_parts.3.refs_0_), channel_id=1, source_target_pairs={{0,48},{16,0},{32,16},{48,32},{1,49},{17,1},{33,17},{49,33},{2,50}... | collective-permute-start | bytes 147464 | tf_op jit(solution)/shard_map/ppermute | solution.py:287
  62.8 7.8 %collective-permute-start.10 = (f32[24,512]{1,0:T(8,128)S(1)}, f32[24,512]{1,0:T(8,128)S(1)}, u32[]{:S(2)}, u32[]{:S(2)}) collective-permute-start(f32[24,512]{1,0:T(8,128)S(1)} %ring_sum.1.refs_0_), channel_id=1, source_target_pairs={{0,128},{64,192},{128,0},{192,64},{1,129},{65,193},{129,1},{193,65... | collective-permute-start | bytes 147464 | tf_op jit(solution)/shard_map/ppermute | solution.py:287
  65.9 6.2 %collective-permute-start.8 = (f32[24,512]{1,0:T(8,128)S(1)}, f32[24,512]{1,0:T(8,128)S(1)}, u32[]{:S(2)}, u32[]{:S(2)}) collective-permute-start(f32[24,512]{1,0:T(8,128)S(1)} %ring_sum.1.refs_0_), channel_id=1, source_target_pairs={{0,64},{64,128},{128,192},{192,0},{1,65},{65,129},{129,193},{193,1... | collective-permute-start | bytes 147464 | tf_op jit(solution)/shard_map/ppermute | solution.py:287
  67.1 5.0 %collective-permute-start.9 = (f32[24,512]{1,0:T(8,128)S(1)}, f32[24,512]{1,0:T(8,128)S(1)}, u32[]{:S(2)}, u32[]{:S(2)}) collective-permute-start(f32[24,512]{1,0:T(8,128)S(1)} %ring_sum.1.refs_0_), channel_id=1, source_target_pairs={{0,192},{64,0},{128,64},{192,128},{1,193},{65,1},{129,65},{193,129... | collective-permute-start | bytes 147464 | tf_op jit(solution)/shard_map/ppermute | solution.py:287
  72.9 12.5 %all-to-all-start.3 = ((f32[8,24,512]{2,1,0:T(8,128)}), f32[8,24,512]{2,1,0:T(8,128)S(1)}, u32[]{:S(2)}, u32[]{:S(2)}) async-start(f32[8,24,512]{2,1,0:T(8,128)} %bitcast.13), calls=%async_computation.3 | async-start | bytes 786432 | tf_op jit(solution)/shard_map/all_to_all | solution.py:283
  78.8 10.6 %collective-permute-start.4 = (f32[512,512]{1,0:T(8,128)S(1)}, f32[512,512]{1,0:T(8,128)S(1)}, u32[]{:S(2)}, u32[]{:S(2)}) collective-permute-start(f32[512,512]{1,0:T(8,128)S(1)} %bitcast.15), channel_id=1, source_target_pairs={{0,1},{1,0},{2,3},{3,2},{4,5},{5,4},{6,7},{7,6},{8,9},{9,8},{10,11... | collective-permute-start | bytes 3145736 | tf_op jit(solution)/shard_map/ppermute | solution.py:359
  85.4 6.0 %collective-permute-start.11 = (f32[192,512]{1,0:T(8,128)S(1)}, f32[192,512]{1,0:T(8,128)S(1)}, u32[]{:S(2)}, u32[]{:S(2)}) collective-permute-start(f32[192,512]{1,0:T(8,128)S(1)} %bitcast.18), channel_id=1, source_target_pairs={{0,1},{1,0},{2,3},{3,2},{4,5},{5,4},{6,7},{7,6},{8,9},{9,8},{10,11... | collective-permute-start | bytes 1179656 | tf_op jit(solution)/shard_map/ppermute | solution.py:360

commit v3 on v2

--- a/solution.py
+++ b/solution.py
@@ -16,7 +16,7 @@
 W = 2 * B
 CH = 64
 CHIPS = 8
-STEPS = 2
+STEPS = 1
 ROWS = 1024
 HALF = 3 * B // 2
 GR = HALF // CHIPS // 2
@@ -109,12 +109,17 @@
         copy.wait()
 
 
-def keep_kernel(s_ref, zh_ref, zl_ref, got_ref, p_ref):
-    per = CHIPS // STEPS
+def keep_kernel(s_ref, zh_ref, zl_ref, got_ref, p_hbm, p_ref, sems):
+    per = CHIPS // 2
     z = (zh_ref[...], zl_ref[...])
-    for i in range(STEPS):
+    copies = []
+    for i in range(2):
         rows = pl.ds(i * per * CH, per * CH)
         p_ref[rows, :] = got_ref[rows, :] + product_rows(s_ref, i * per, (i + 1) * per, z)
+        copies.append(pltpu.make_async_copy(p_ref.at[rows], p_hbm.at[rows], sems.at[i]))
+        copies[i].start()
+    for copy in copies:
+        copy.wait()
 
 
 def products(where, sigma, two, one, top, b2, b1):
@@ -145,8 +150,9 @@
     pair = pl.pallas_call(
         keep_kernel,
         in_specs=[VM] * 4,
-        out_specs=VM,
+        out_specs=HBM,
         out_shape=shape_p,
+        scratch_shapes=[pltpu.VMEM(shape_p.shape, F32), pltpu.SemaphoreType.DMA((2,))],
         compiler_params=PARAMS,
         cost_estimate=LONG,
         name="product_keep",

time: 93.4 us -> 93 us (level)
  no operation moved by 1% of the time
where the time goes in v3:
time: 93 us; the launch traced here: 92.7 us
  starting transfers between devices  47.7 us (51%)
  waiting for transfers between devices  26.9 us (29%)
  Pallas kernels  17 us (18%)
    all_to_all x4, starting transfers between devices, a2a(): return lax.all_to_all(value, axes, 0, 0, tiled=True)  22.6 us
    all_to_all x4, waiting for transfers between devices, a2a(): return lax.all_to_all(value, axes, 0, 0, tiled=True)  21.4 us
    ppermute x6, starting transfers between devices, ring(): lax.ppermute(value, axis, [(i, (i + k) % 4) for i in range(4)])  10.9 us
    pallas_call x1, Pallas kernels, products(): pl.pallas_call(send_kernel, in_specs=[SM] + [HBM] * 6, out_specs=[VM] * 5...  5.34 us
    ppermute x6, waiting for transfers between devices, ring(): lax.ppermute(value, axis, [(i, (i + k) % 4) for i in range(4)])  4.24 us
    ppermute x1, starting transfers between devices, per_device(): g_oth = lax.ppermute(g, 'c', SWAP)  4.02 us
    ppermute x1, starting transfers between devices, products(): got = lax.ppermute(send, 'c', SWAP)  3.33 us
    ppermute x1, starting transfers between devices, per_device(): lax.ppermute(chunks, 'c', SWAP)  2.87 us
  transfers between devices with their start and end apart: 16, of which 9 were waited for; matrix products, arithmetic and copies ran while one was open for 0% of the time, Pallas kernels for 9%

profile of v3, /device:TPU:1, one launch (start us, length us, event | category | flops | bytes accessed | tf_op | source)
XLA Modules:
  0.0 92.7 jit_solution(10625644960221935745)
XLA Ops:
  0.8 0.1 pad_add_fusion.w_ref
  0.9 5.3 %product_send.1 = (f32[512,512]{1,0:T(8,128)S(1)}, bf16[1024,512]{1,0:T(8,128)(2,1)S(1)}, bf16[1024,512]{1,0:T(8,128)(2,1)S(1)}, f32[8,64,1024]{2,1,0:T(8,128)S(1)}, f32[64,512]{1,0:T(8,128)S(1)}) custom-call(s32[4]{0:T(128)S(1)} %pad_add_fusion.w_ref, f32[8,128,1024]{2,1,0:T(8,128)} %bitcast.27, f32[1024,256]{1,0:T(8,128)} %two_hbm.1, f32[1024,256]{1,0:T(8,128)} %one_hbm.1, ...), custom_call_target="tpu_custom_call" | custom-call | flops 21474836480 | bytes 8388608 | tf_op jit(solution)/shard_map/product_send/pallas_call | solution.py:130
  6.2 3.3 %collective-permute-start = (f32[512,512]{1,0:T(8,128)S(1)}, f32[512,512]{1,0:T(8,128)S(1)}, u32[]{:S(2)}, u32[]{:S(2)}) collective-permute-start(f32[512,512]{1,0:T(8,128)S(1)} %get-tuple-element.26), channel_id=1, source_target_pairs={{0,1},{1,0},{2,3},{3,2},{4,5},{5,4},{6,7},{7,6},{8,9},{9,8},{10,11... | collective-permute-start | bytes 3145736 | tf_op jit(solution)/shard_map/ppermute | solution.py:149
  9.5 2.0 %collective-permute-start.1 = (f32[64,512]{1,0:T(8,128)S(1)}, f32[64,512]{1,0:T(8,128)S(1)}, u32[]{:S(2)}, u32[]{:S(2)}) collective-permute-start(f32[64,512]{1,0:T(8,128)S(1)} %get-tuple-element.27), channel_id=1, source_target_pairs={{0,5},{1,21},{2,36},{3,52},{4,67},{5,84},{6,102},{7,117},{8,131},{... | collective-permute-start | bytes 393224 | tf_op jit(solution)/shard_map/ppermute | solution.py:310
  11.6 0.3 collective-permute-done.got_ref
  11.8 0.0 copy-start.1
  11.8 0.0 copy-start.3
  11.8 0.0 copy-start.4
  11.8 2.7 %product_keep.1 = f32[512,512]{1,0:T(8,128)} custom-call(f32[8,64,1024]{2,1,0:T(8,128)S(1)} %get-tuple-element.23.s_ref, bf16[1024,512]{1,0:T(8,128)(2,1)S(1)} %get-tuple-element.24.zh_ref, bf16[1024,512]{1,0:T(8,128)(2,1)S(1)} %get-tuple-element.25.zl_ref, f32[512,512]{1,0:T(8,128)S(1)} %collective-permute-done.got_ref), custom_call_target="tpu_custom_call" | custom-call | flops 21474836480 | bytes 8388608 | tf_op jit(solution)/shard_map/product_keep/pallas_call | solution.py:150
  14.5 8.6 %all-to-all-start = ((f32[8,64,512]{2,1,0:T(8,128)}), f32[8,64,512]{2,1,0:T(8,128)S(1)}, u32[]{:S(2)}, u32[]{:S(2)}) async-start(f32[8,64,512]{2,1,0:T(8,128)} %bitcast.7), calls=%async_computation | async-start | bytes 2097152 | tf_op jit(solution)/shard_map/all_to_all | solution.py:289
  23.1 0.0 copy-start
  23.1 0.0 copy-start.2
  23.1 0.0 collective-permute-done.1.z_ref
  23.1 0.0 copy-done.1
  23.1 0.0 copy-done.3
  23.1 0.0 copy-done.4
  23.1 0.8 panel_rows.1.after_ref.z_own_ref
  24.0 1.0 %collective-permute-start.3 = (f32[64,512]{1,0:T(8,128)S(1)}, f32[64,512]{1,0:T(8,128)S(1)}, u32[]{:S(2)}, u32[]{:S(2)}) collective-permute-start(f32[64,512]{1,0:T(8,128)S(1)} %panel_rows.1.after_ref.z_own_ref), channel_id=1, source_target_pairs={{0,1},{1,0},{2,3},{3,2},{4,5},{5,4},{6,7},{7,6},{8,9},{9,8},{10,11... | collective-permute-start | bytes 393224 | tf_op jit(solution)/shard_map/ppermute | solution.py:321
  25.0 13.0 %all-to-all-done = f32[8,64,512]{2,1,0:T(8,128)S(1)} async-done(((f32[8,64,512]{2,1,0:T(8,128)}), f32[8,64,512]{2,1,0:T(8,128)S(1)}, u32[]{:S(2)}, u32[]{:S(2)}) %all-to-all-start) | async-done | bytes 1048608 | tf_op jit(solution)/shard_map/all_to_all | solution.py:289
  38.0 0.1 sum_parts.2.own_ref
  38.1 0.9 %collective-permute-start.2 = (f32[64,512]{1,0:T(8,128)S(1)}, f32[64,512]{1,0:T(8,128)S(1)}, u32[]{:S(2)}, u32[]{:S(2)}) collective-permute-start(f32[64,512]{1,0:T(8,128)S(1)} %sum_parts.2.own_ref), channel_id=1, source_target_pairs={{0,1},{1,0},{2,3},{3,2},{4,5},{5,4},{6,7},{7,6},{8,9},{9,8},{10,11... | collective-permute-start | bytes 393224 | tf_op jit(solution)/shard_map/ppermute | solution.py:323
  39.0 0.0 collective-permute-done.3.z_oth_ref
  39.0 1.0 %collective-permute-done.2.oth_ref = f32[64,512]{1,0:T(8,128)S(1)} collective-permute-done((f32[64,512]{1,0:T(8,128)S(1)}, f32[64,512]{1,0:T(8,128)S(1)}, u32[]{:S(2)}, u32[]{:S(2)}) %collective-permute-start.2) | collective-permute-done | bytes 131104 | tf_op jit(solution)/shard_map/ppermute | solution.py:323
  40.0 1.7 %gram.1 = f32[192,512]{1,0:T(8,128)} custom-call(s32[4]{0:T(128)S(1)} %pad_add_fusion.w_ref, f32[64,512]{1,0:T(8,128)S(1)} %sum_parts.2.own_ref, f32[64,512]{1,0:T(8,128)S(1)} %collective-permute-done.2.oth_ref, f32[64,512]{1,0:T(8,128)S(1)} %panel_rows.1.after_ref.z_own_ref, f32[64,512]{1,0:T(8,128)S(1)} %collective-permute-done.3.z_oth_ref), custom_call_target="tpu_custom_call" | custom-call | tf_op jit(solution)/shard_map/gram/pallas_call | solution.py:325
  41.7 3.5 %all-to-all-start.2 = ((f32[8,24,512]{2,1,0:T(8,128)}), f32[8,24,512]{2,1,0:T(8,128)S(1)}, u32[]{:S(2)}, u32[]{:S(2)}) async-start(f32[8,24,512]{2,1,0:T(8,128)} %bitcast.11), calls=%async_computation.2 | async-start | bytes 786432 | tf_op jit(solution)/shard_map/all_to_all | solution.py:289
  45.1 0.0 copy-done
  45.1 0.0 copy-done.2
  45.1 2.1 %chunks.1 = (f32[512,512]{1,0:T(8,128)}, f32[256,256]{1,0:T(8,128)S(1)}, f32[256,256]{1,0:T(8,128)S(1)}) custom-call(s32[4]{0:T(128)S(1)} %pad_add_fusion.w_ref, f32[64,512]{1,0:T(8,128)S(1)} %sum_parts.2.own_ref, s32[1,48]{1,0:T(1,128)S(1)} %bitcast.23, s32[1,32]{1,0:T(1,128)S(1)} %bitcast.26, f32[256,256]{1,0:T(8,128)S(1)} %copy-done.1, ...), custom_call_target="tpu_custom_call" | custom-call | tf_op jit(solution)/shard_map/chunks/pallas_call | solution.py:336
  47.3 4.7 %all-to-all-done.2 = f32[8,24,512]{2,1,0:T(8,128)S(1)} async-done(((f32[8,24,512]{2,1,0:T(8,128)}), f32[8,24,512]{2,1,0:T(8,128)S(1)}, u32[]{:S(2)}, u32[]{:S(2)}) %all-to-all-start.2) | async-done | bytes 393248 | tf_op jit(solution)/shard_map/all_to_all | solution.py:289
  52.0 4.6 %all-to-all-start.1 = ((f32[8,64,512]{2,1,0:T(8,128)}), f32[8,64,512]{2,1,0:T(8,128)S(1)}, u32[]{:S(2)}, u32[]{:S(2)}) async-start(f32[8,64,512]{2,1,0:T(8,128)} %bitcast.9), calls=%async_computation.1 | async-start | bytes 2097152 | tf_op jit(solution)/shard_map/all_to_all | solution.py:289
  56.6 1.5 %collective-permute-start.5 = (f32[24,512]{1,0:T(8,128)S(1)}, f32[24,512]{1,0:T(8,128)S(1)}, u32[]{:S(2)}, u32[]{:S(2)}) collective-permute-start(f32[24,512]{1,0:T(8,128)S(1)} %sum_parts.3.refs_0_), channel_id=1, source_target_pairs={{0,32},{16,48},{32,0},{48,16},{1,33},{17,49},{33,1},{49,17},{2,34}... | collective-permute-start | bytes 147464 | tf_op jit(solution)/shard_map/ppermute | solution.py:293
  58.1 0.5 collective-permute-start.6
  58.6 2.2 %collective-permute-start.7 = (f32[24,512]{1,0:T(8,128)S(1)}, f32[24,512]{1,0:T(8,128)S(1)}, u32[]{:S(2)}, u32[]{:S(2)}) collective-permute-start(f32[24,512]{1,0:T(8,128)S(1)} %sum_parts.3.refs_0_), channel_id=1, source_target_pairs={{0,48},{16,0},{32,16},{48,32},{1,49},{17,1},{33,17},{49,33},{2,50}... | collective-permute-start | bytes 147464 | tf_op jit(solution)/shard_map/ppermute | solution.py:293
  60.8 0.4 collective-permute-done.5.refs_1_
  61.2 1.3 %collective-permute-done.6.refs_2_ = f32[24,512]{1,0:T(8,128)S(1)} collective-permute-done((f32[24,512]{1,0:T(8,128)S(1)}, f32[24,512]{1,0:T(8,128)S(1)}, u32[]{:S(2)}, u32[]{:S(2)}) %collective-permute-start.6) | collective-permute-done | bytes 49184 | tf_op jit(solution)/shard_map/ppermute | solution.py:293
  62.4 0.0 collective-permute-done.7.refs_3_
  62.4 3.2 %collective-permute-start.10 = (f32[24,512]{1,0:T(8,128)S(1)}, f32[24,512]{1,0:T(8,128)S(1)}, u32[]{:S(2)}, u32[]{:S(2)}) collective-permute-start(f32[24,512]{1,0:T(8,128)S(1)} %ring_sum.1.refs_0_), channel_id=1, source_target_pairs={{0,128},{64,192},{128,0},{192,64},{1,129},{65,193},{129,1},{193,65... | collective-permute-start | bytes 147464 | tf_op jit(solution)/shard_map/ppermute | solution.py:293
  65.6 1.2 %collective-permute-start.8 = (f32[24,512]{1,0:T(8,128)S(1)}, f32[24,512]{1,0:T(8,128)S(1)}, u32[]{:S(2)}, u32[]{:S(2)}) collective-permute-start(f32[24,512]{1,0:T(8,128)S(1)} %ring_sum.1.refs_0_), channel_id=1, source_target_pairs={{0,64},{64,128},{128,192},{192,0},{1,65},{65,129},{129,193},{193,1... | collective-permute-start | bytes 147464 | tf_op jit(solution)/shard_map/ppermute | solution.py:293
  66.8 2.4 %collective-permute-start.9 = (f32[24,512]{1,0:T(8,128)S(1)}, f32[24,512]{1,0:T(8,128)S(1)}, u32[]{:S(2)}, u32[]{:S(2)}) collective-permute-start(f32[24,512]{1,0:T(8,128)S(1)} %ring_sum.1.refs_0_), channel_id=1, source_target_pairs={{0,192},{64,0},{128,64},{192,128},{1,193},{65,1},{129,65},{193,129... | collective-permute-start | bytes 147464 | tf_op jit(solution)/shard_map/ppermute | solution.py:293
  69.2 1.1 %collective-permute-done.10.refs_3_ = f32[24,512]{1,0:T(8,128)S(1)} collective-permute-done((f32[24,512]{1,0:T(8,128)S(1)}, f32[24,512]{1,0:T(8,128)S(1)}, u32[]{:S(2)}, u32[]{:S(2)}) %collective-permute-start.10) | collective-permute-done | bytes 49184 | tf_op jit(solution)/shard_map/ppermute | solution.py:293
  70.2 1.6 %collective-permute-done.8.refs_1_ = f32[24,512]{1,0:T(8,128)S(1)} collective-permute-done((f32[24,512]{1,0:T(8,128)S(1)}, f32[24,512]{1,0:T(8,128)S(1)}, u32[]{:S(2)}, u32[]{:S(2)}) %collective-permute-start.8) | collective-permute-done | bytes 49184 | tf_op jit(solution)/shard_map/ppermute | solution.py:293
  71.8 0.0 collective-permute-done.9.refs_2_
  71.8 0.8 spread.1
  72.6 0.0 all-to-all-done.1
  72.6 5.9 %all-to-all-start.3 = ((f32[8,24,512]{2,1,0:T(8,128)}), f32[8,24,512]{2,1,0:T(8,128)S(1)}, u32[]{:S(2)}, u32[]{:S(2)}) async-start(f32[8,24,512]{2,1,0:T(8,128)} %bitcast.13), calls=%async_computation.3 | async-start | bytes 786432 | tf_op jit(solution)/shard_map/all_to_all | solution.py:289
  78.5 2.9 %collective-permute-start.4 = (f32[512,512]{1,0:T(8,128)S(1)}, f32[512,512]{1,0:T(8,128)S(1)}, u32[]{:S(2)}, u32[]{:S(2)}) collective-permute-start(f32[512,512]{1,0:T(8,128)S(1)} %bitcast.15), channel_id=1, source_target_pairs={{0,1},{1,0},{2,3},{3,2},{4,5},{5,4},{6,7},{7,6},{8,9},{9,8},{10,11... | collective-permute-start | bytes 3145736 | tf_op jit(solution)/shard_map/ppermute | solution.py:365
  81.4 3.7 %all-to-all-done.3 = f32[8,24,512]{2,1,0:T(8,128)S(1)} async-done(((f32[8,24,512]{2,1,0:T(8,128)}), f32[8,24,512]{2,1,0:T(8,128)S(1)}, u32[]{:S(2)}, u32[]{:S(2)}) %all-to-all-start.3) | async-done | bytes 393248 | tf_op jit(solution)/shard_map/all_to_all | solution.py:289
  85.1 4.0 %collective-permute-start.11 = (f32[192,512]{1,0:T(8,128)S(1)}, f32[192,512]{1,0:T(8,128)S(1)}, u32[]{:S(2)}, u32[]{:S(2)}) collective-permute-start(f32[192,512]{1,0:T(8,128)S(1)} %bitcast.18), channel_id=1, source_target_pairs={{0,1},{1,0},{2,3},{3,2},{4,5},{5,4},{6,7},{7,6},{8,9},{9,8},{10,11... | collective-permute-start | bytes 1179656 | tf_op jit(solution)/shard_map/ppermute | solution.py:366
  89.1 0.0 collective-permute-done.4.oth_ref
  89.1 2.0 %assemble.1 = (f32[1024,256]{1,0:T(8,128)}, f32[1024,256]{1,0:T(8,128)}) custom-call(s32[4]{0:T(128)S(1)} %pad_add_fusion.w_ref, f32[512,512]{1,0:T(8,128)S(1)} %bitcast.16, f32[512,512]{1,0:T(8,128)S(1)} %collective-permute-done.4.oth_ref), custom_call_target="tpu_custom_call" | custom-call | tf_op jit(solution)/shard_map/assemble/pallas_call | solution.py:358
  91.1 0.0 collective-permute-done.11.oth_ref
  91.1 1.5 %last.1 = (f32[256,256]{1,0:T(8,128)}, f32[256,256]{1,0:T(8,128)}, f32[256,256]{1,0:T(8,128)}) custom-call(s32[4]{0:T(128)S(1)} %pad_add_fusion.w_ref, f32[192,512]{1,0:T(8,128)S(1)} %bitcast.19, f32[192,512]{1,0:T(8,128)S(1)} %collective-permute-done.11.oth_ref, f32[256,256]{1,0:T(8,128)S(1)} %copy-done, f32[256,256]{1,0:T(8,128)S(1)} %get-tuple-element.35.it_ref, ...), custom_call_target="tpu_custom_call" | custom-call | tf_op jit(solution)/shard_map/last/pallas_call | solution.py:368
  (2 shorter events, 0.0 us)
Async XLA Ops:
  6.2 5.6 %collective-permute-start = (f32[512,512]{1,0:T(8,128)S(1)}, f32[512,512]{1,0:T(8,128)S(1)}, u32[]{:S(2)}, u32[]{:S(2)}) collective-permute-start(f32[512,512]{1,0:T(8,128)S(1)} %get-tuple-element.26), channel_id=1, source_target_pairs={{0,1},{1,0},{2,3},{3,2},{4,5},{5,4},{6,7},{7,6},{8,9},{9,8},{10,11... | collective-permute-start | bytes 3145736 | tf_op jit(solution)/shard_map/ppermute | solution.py:149
  9.5 13.6 %collective-permute-start.1 = (f32[64,512]{1,0:T(8,128)S(1)}, f32[64,512]{1,0:T(8,128)S(1)}, u32[]{:S(2)}, u32[]{:S(2)}) collective-permute-start(f32[64,512]{1,0:T(8,128)S(1)} %get-tuple-element.27), channel_id=1, source_target_pairs={{0,5},{1,21},{2,36},{3,52},{4,67},{5,84},{6,102},{7,117},{8,131},{... | collective-permute-start | bytes 393224 | tf_op jit(solution)/shard_map/ppermute | solution.py:310
  11.8 11.3 %copy-start.1 = (f32[256,256]{1,0:T(8,128)S(1)}, f32[256,256]{1,0:T(8,128)}, u32[]{:S(2)}) copy-start(f32[256,256]{1,0:T(8,128)} %top_ref.3) | copy-start | bytes 786436
  11.8 11.3 %copy-start.3 = (s32[48]{0:T(128)S(1)}, s32[48]{0:T(128)}, u32[]{:S(2)}) copy-start(s32[48]{0:T(128)} %param.12) | copy-start | bytes 580
  11.8 11.3 %copy-start.4 = (s32[32]{0:T(128)S(1)}, s32[32]{0:T(128)}, u32[]{:S(2)}) copy-start(s32[32]{0:T(128)} %param.13) | copy-start | bytes 388
  14.5 23.5 %all-to-all-start = ((f32[8,64,512]{2,1,0:T(8,128)}), f32[8,64,512]{2,1,0:T(8,128)S(1)}, u32[]{:S(2)}, u32[]{:S(2)}) async-start(f32[8,64,512]{2,1,0:T(8,128)} %bitcast.7), calls=%async_computation | async-start | bytes 2097152 | tf_op jit(solution)/shard_map/all_to_all | solution.py:289
  23.1 22.0 %copy-start = (f32[256,256]{1,0:T(8,128)S(1)}, f32[256,256]{1,0:T(8,128)}, u32[]{:S(2)}) copy-start(f32[256,256]{1,0:T(8,128)} %inv2_ref.3) | copy-start | bytes 786436
  23.1 22.0 %copy-start.2 = (f32[256,256]{1,0:T(8,128)S(1)}, f32[256,256]{1,0:T(8,128)}, u32[]{:S(2)}) copy-start(f32[256,256]{1,0:T(8,128)} %inv1_ref.1) | copy-start | bytes 786436
  24.0 15.0 %collective-permute-start.3 = (f32[64,512]{1,0:T(8,128)S(1)}, f32[64,512]{1,0:T(8,128)S(1)}, u32[]{:S(2)}, u32[]{:S(2)}) collective-permute-start(f32[64,512]{1,0:T(8,128)S(1)} %panel_rows.1.after_ref.z_own_ref), channel_id=1, source_target_pairs={{0,1},{1,0},{2,3},{3,2},{4,5},{5,4},{6,7},{7,6},{8,9},{9,8},{10,11... | collective-permute-start | bytes 393224 | tf_op jit(solution)/shard_map/ppermute | solution.py:321
  38.1 1.9 %collective-permute-start.2 = (f32[64,512]{1,0:T(8,128)S(1)}, f32[64,512]{1,0:T(8,128)S(1)}, u32[]{:S(2)}, u32[]{:S(2)}) collective-permute-start(f32[64,512]{1,0:T(8,128)S(1)} %sum_parts.2.own_ref), channel_id=1, source_target_pairs={{0,1},{1,0},{2,3},{3,2},{4,5},{5,4},{6,7},{7,6},{8,9},{9,8},{10,11... | collective-permute-start | bytes 393224 | tf_op jit(solution)/shard_map/ppermute | solution.py:323
  41.7 10.3 %all-to-all-start.2 = ((f32[8,24,512]{2,1,0:T(8,128)}), f32[8,24,512]{2,1,0:T(8,128)S(1)}, u32[]{:S(2)}, u32[]{:S(2)}) async-start(f32[8,24,512]{2,1,0:T(8,128)} %bitcast.11), calls=%async_computation.2 | async-start | bytes 786432 | tf_op jit(solution)/shard_map/all_to_all | solution.py:289
  52.0 20.6 %all-to-all-start.1 = ((f32[8,64,512]{2,1,0:T(8,128)}), f32[8,64,512]{2,1,0:T(8,128)S(1)}, u32[]{:S(2)}, u32[]{:S(2)}) async-start(f32[8,64,512]{2,1,0:T(8,128)} %bitcast.9), calls=%async_computation.1 | async-start | bytes 2097152 | tf_op jit(solution)/shard_map/all_to_all | solution.py:289
  56.6 4.5 %collective-permute-start.5 = (f32[24,512]{1,0:T(8,128)S(1)}, f32[24,512]{1,0:T(8,128)S(1)}, u32[]{:S(2)}, u32[]{:S(2)}) collective-permute-start(f32[24,512]{1,0:T(8,128)S(1)} %sum_parts.3.refs_0_), channel_id=1, source_target_pairs={{0,32},{16,48},{32,0},{48,16},{1,33},{17,49},{33,1},{49,17},{2,34}... | collective-permute-start | bytes 147464 | tf_op jit(solution)/shard_map/ppermute | solution.py:293
  58.1 4.3 %collective-permute-start.6 = (f32[24,512]{1,0:T(8,128)S(1)}, f32[24,512]{1,0:T(8,128)S(1)}, u32[]{:S(2)}, u32[]{:S(2)}) collective-permute-start(f32[24,512]{1,0:T(8,128)S(1)} %sum_parts.3.refs_0_), channel_id=1, source_target_pairs={{0,16},{16,32},{32,48},{48,0},{1,17},{17,33},{33,49},{49,1},{2,18}... | collective-permute-start | bytes 147464 | tf_op jit(solution)/shard_map/ppermute | solution.py:293
  58.6 3.8 %collective-permute-start.7 = (f32[24,512]{1,0:T(8,128)S(1)}, f32[24,512]{1,0:T(8,128)S(1)}, u32[]{:S(2)}, u32[]{:S(2)}) collective-permute-start(f32[24,512]{1,0:T(8,128)S(1)} %sum_parts.3.refs_0_), channel_id=1, source_target_pairs={{0,48},{16,0},{32,16},{48,32},{1,49},{17,1},{33,17},{49,33},{2,50}... | collective-permute-start | bytes 147464 | tf_op jit(solution)/shard_map/ppermute | solution.py:293
  62.4 7.8 %collective-permute-start.10 = (f32[24,512]{1,0:T(8,128)S(1)}, f32[24,512]{1,0:T(8,128)S(1)}, u32[]{:S(2)}, u32[]{:S(2)}) collective-permute-start(f32[24,512]{1,0:T(8,128)S(1)} %ring_sum.1.refs_0_), channel_id=1, source_target_pairs={{0,128},{64,192},{128,0},{192,64},{1,129},{65,193},{129,1},{193,65... | collective-permute-start | bytes 147464 | tf_op jit(solution)/shard_map/ppermute | solution.py:293
  65.6 6.2 %collective-permute-start.8 = (f32[24,512]{1,0:T(8,128)S(1)}, f32[24,512]{1,0:T(8,128)S(1)}, u32[]{:S(2)}, u32[]{:S(2)}) collective-permute-start(f32[24,512]{1,0:T(8,128)S(1)} %ring_sum.1.refs_0_), channel_id=1, source_target_pairs={{0,64},{64,128},{128,192},{192,0},{1,65},{65,129},{129,193},{193,1... | collective-permute-start | bytes 147464 | tf_op jit(solution)/shard_map/ppermute | solution.py:293
  66.8 5.0 %collective-permute-start.9 = (f32[24,512]{1,0:T(8,128)S(1)}, f32[24,512]{1,0:T(8,128)S(1)}, u32[]{:S(2)}, u32[]{:S(2)}) collective-permute-start(f32[24,512]{1,0:T(8,128)S(1)} %ring_sum.1.refs_0_), channel_id=1, source_target_pairs={{0,192},{64,0},{128,64},{192,128},{1,193},{65,1},{129,65},{193,129... | collective-permute-start | bytes 147464 | tf_op jit(solution)/shard_map/ppermute | solution.py:293
  72.6 12.5 %all-to-all-start.3 = ((f32[8,24,512]{2,1,0:T(8,128)}), f32[8,24,512]{2,1,0:T(8,128)S(1)}, u32[]{:S(2)}, u32[]{:S(2)}) async-start(f32[8,24,512]{2,1,0:T(8,128)} %bitcast.13), calls=%async_computation.3 | async-start | bytes 786432 | tf_op jit(solution)/shard_map/all_to_all | solution.py:289
  78.5 10.6 %collective-permute-start.4 = (f32[512,512]{1,0:T(8,128)S(1)}, f32[512,512]{1,0:T(8,128)S(1)}, u32[]{:S(2)}, u32[]{:S(2)}) collective-permute-start(f32[512,512]{1,0:T(8,128)S(1)} %bitcast.15), channel_id=1, source_target_pairs={{0,1},{1,0},{2,3},{3,2},{4,5},{5,4},{6,7},{7,6},{8,9},{9,8},{10,11... | collective-permute-start | bytes 3145736 | tf_op jit(solution)/shard_map/ppermute | solution.py:365
  85.1 6.0 %collective-permute-start.11 = (f32[192,512]{1,0:T(8,128)S(1)}, f32[192,512]{1,0:T(8,128)S(1)}, u32[]{:S(2)}, u32[]{:S(2)}) collective-permute-start(f32[192,512]{1,0:T(8,128)S(1)} %bitcast.18), channel_id=1, source_target_pairs={{0,1},{1,0},{2,3},{3,2},{4,5},{5,4},{6,7},{7,6},{8,9},{9,8},{10,11... | collective-permute-start | bytes 1179656 | tf_op jit(solution)/shard_map/ppermute | solution.py:366
